TPU v7x, 256 devices: a whole 4x4x8 slice. The times are simulated.
256 devices in a mesh: dom: 64 (over z, y, x_hi), chan: 4 (over x_lo, core).
Axes of the slice: x: 4 (x_hi: 2, x_lo: 2; x = x_hi * 2 + x_lo), y: 4, z: 8, core: 2. Of those that a mesh axis runs over, the one named last changes fastest.
Arguments:
- node_latent: bfloat16 [163840, 256], P('dom', 'chan'), may hold values from -6 to 6
- edge_latent: bfloat16 [1376256, 256], P(('dom', 'chan')), may hold values from -6 to 6
- senders: int32 [1376256], P(('dom', 'chan')), may hold values from 0 to 2559
- receivers: int32 [1376256], P(('dom', 'chan')), may hold values from 0 to 4607
- edge_count: int32 [64], P('dom'), may hold values from 7168 to 21504, as said below
- send_list: int32 [64, 64, 32], P('dom'), may hold values from 0 to 2559
- w_edge_in: bfloat16 [768, 256], replicated, may hold values from -0.21875 to 0.21875
- edge_in_bias: float32 [256], replicated, may hold values from -3 to 3
- w_edge_out: bfloat16 [256, 256], replicated, may hold values from -0.375 to 0.375
- edge_out_bias: float32 [256], replicated, may hold values from -3 to 3
- edge_gain: float32 [256], replicated, may hold values from 0.1 to 1.9
- edge_shift: float32 [256], replicated, may hold values from -3 to 3
- w_node_in: bfloat16 [512, 256], P(None, 'chan'), may hold values from -0.25 to 0.25
- node_in_bias: bfloat16 [256], P('chan'), may hold values from -3 to 3
- w_node_out: bfloat16 [256, 256], P('chan'), may hold values from -0.375 to 0.375
- node_out_bias: float32 [256], replicated, may hold values from -3 to 3
- node_gain: float32 [256], P('chan'), may hold values from 0.1 to 1.9
- node_shift: float32 [256], P('chan'), may hold values from -3 to 3
Outputs:
- node_new: bfloat16 [163840, 256], P('dom', 'chan')
- edge_new: bfloat16 [1376256, 256], P(('dom', 'chan'))
Inputs may be any that keep to these rules, and one draw needn't show every extreme that they name: `senders`: edge blocks belong to the sender's partition. `edge_count`: some partition's block is full in every draw.
All inputs are finite; a program needn't handle non-finite values.
Results may differ from a plain program's by a relative error of at most 0.012.
Values may be sent and summed in bfloat16 or wider, within the bound.
A program may use at most 128 MiB of HBM per device.

v0:
```python
import jax
import jax.numpy as jnp
from jax import lax
from jax.sharding import PartitionSpec as P


def silu_rows(values):
    return values * jax.nn.sigmoid(values)


def body(
    node_latent,
    edge_latent,
    senders,
    receivers,
    edge_count,
    send_list,
    w_edge_in,
    edge_in_bias,
    w_edge_out,
    edge_out_bias,
    edge_gain,
    edge_shift,
    w_node_in,
    node_in_bias,
    w_node_out,
    node_out_bias,
    node_gain,
    node_shift,
):
    node_rows, quarter = node_latent.shape
    latent = w_edge_out.shape[0]
    part_count = lax.axis_size("dom")
    send_rows = send_list[0]
    slot_count = send_rows.shape[1]
    chan_index = lax.axis_index("chan")
    outgoing = node_latent[send_rows.reshape(-1)].reshape(part_count, slot_count, quarter)
    incoming = lax.all_to_all(outgoing, "dom", split_axis=0, concat_axis=0, tiled=True)
    table = jnp.concatenate(
        [node_latent, incoming.reshape(part_count * slot_count, quarter)], axis=0
    )
    table = lax.all_gather(table, "chan", axis=1, tiled=True)
    edge_rows = edge_latent.shape[0]
    slot_index = chan_index * edge_rows + jnp.arange(edge_rows, dtype=jnp.int32)
    live_mask = (slot_index < edge_count[0]).astype(jnp.float32)[:, None]
    sender_feats = table[senders]
    receiver_feats = table[receivers]
    pre_edge = jnp.dot(edge_latent, w_edge_in[:latent], preferred_element_type=jnp.float32)
    pre_edge = pre_edge + jnp.dot(
        sender_feats, w_edge_in[latent : 2 * latent], preferred_element_type=jnp.float32
    )
    pre_edge = pre_edge + jnp.dot(
        receiver_feats, w_edge_in[2 * latent :], preferred_element_type=jnp.float32
    )
    edge_hidden = silu_rows(pre_edge + edge_in_bias).astype(jnp.bfloat16)
    edge_post = jnp.dot(edge_hidden, w_edge_out, preferred_element_type=jnp.float32) + edge_out_bias
    edge_mean = jnp.mean(edge_post, axis=-1, keepdims=True)
    edge_centred = edge_post - edge_mean
    edge_var = jnp.mean(edge_centred * edge_centred, axis=-1, keepdims=True)
    edge_norm = edge_centred * lax.rsqrt(edge_var + 1e-05) * edge_gain + edge_shift
    edge_new = (edge_latent.astype(jnp.float32) + live_mask * edge_norm).astype(jnp.bfloat16)
    messages = edge_new.astype(jnp.float32) * live_mask
    partial_sums = jax.ops.segment_sum(
        messages, receivers, num_segments=node_rows + part_count * slot_count
    )
    local_part = partial_sums[:node_rows]
    halo_part = partial_sums[node_rows:].reshape(part_count, slot_count, latent)
    returned = lax.all_to_all(
        halo_part.astype(jnp.bfloat16), "dom", split_axis=0, concat_axis=0, tiled=True
    ).astype(halo_part.dtype)
    local_part = local_part + jax.ops.segment_sum(
        returned.reshape(-1, latent), send_rows.reshape(-1), num_segments=node_rows
    )
    own_nodes = table[:node_rows]
    summed = lax.psum(local_part, "chan")
    summed_bf = summed.astype(jnp.bfloat16)
    node_pre = jnp.dot(own_nodes, w_node_in[:latent], preferred_element_type=jnp.float32)
    node_pre = node_pre + jnp.dot(summed_bf, w_node_in[latent:], preferred_element_type=jnp.float32)
    node_hidden = silu_rows(node_pre + node_in_bias.astype(jnp.float32)).astype(jnp.bfloat16)
    node_terms = jnp.dot(node_hidden, w_node_out, preferred_element_type=jnp.float32)
    own_post = lax.psum_scatter(node_terms, "chan", scatter_dimension=1, tiled=True)
    own_post = own_post + lax.dynamic_slice_in_dim(node_out_bias, chan_index * quarter, quarter, 0)
    total_sum, total_square = lax.psum(
        (jnp.sum(own_post, axis=1), jnp.sum(own_post * own_post, axis=1)), "chan"
    )
    row_mean = total_sum / latent
    row_var = total_square / latent - row_mean * row_mean
    node_norm = (own_post - row_mean[:, None]) * lax.rsqrt(row_var + 1e-05)[
        :, None
    ] * node_gain + node_shift
    node_new = (node_latent.astype(jnp.float32) + node_norm).astype(jnp.bfloat16)
    return (node_new, edge_new)


def solution(mesh):
    placed = (
        P("dom", "chan"),
        P(("dom", "chan"), None),
        P(("dom", "chan")),
        P(("dom", "chan")),
        P("dom"),
        P("dom", None, None),
        P(),
        P(),
        P(),
        P(),
        P(),
        P(),
        P(None, "chan"),
        P("chan"),
        P("chan", None),
        P(),
        P("chan"),
        P("chan"),
    )
    return jax.shard_map(
        body,
        mesh=mesh,
        in_specs=placed,
        out_specs=(P("dom", "chan"), P(("dom", "chan"), None)),
        check_vma=False,
    )
```

profile of v0, /device:TPU:1, one launch (start us, length us, event | category | flops | bytes accessed | tf_op | source)
XLA Modules:
  0.0 342.0 jit_solution(13793598128136933142)
XLA Ops:
  7.2 0.0 copy-start
  7.2 0.0 all-gather.2.cloned.1.call-start
  7.2 0.8 copy.40
  8.1 0.1 reshape_squeeze.3
  8.2 1.3 copy.41
  9.5 0.0 copy-start.6
  9.5 8.1 %gather_fusion = bf16[2048,64]{1,0:T(8,128)(2,1)} fusion(bf16[2560,64]{1,0:T(8,128)(2,1)S(1)} %copy.41, s32[2048]{0:T(1024)S(1)} %broadcast_clamp_fusion), kind=kCustom, calls=%fused_computation | custom fusion | bytes 532480 | tf_op jit(solution)/shard_map/gather | solution.py:37
  17.5 1.5 reshape.128
  19.1 27.2 %all_to_all.10 = bf16[64,2,1024]{2,1,0:T(2,128)(2,1)} all-to-all(bf16[64,2,1024]{2,1,0:T(2,128)(2,1)S(1)} %reshape.128), channel_id=1, replica_groups=mesh['dom'=64,'chan'=4] {'dom'}, dimensions={0} | all-to-all | bytes 524288 | tf_op jit(solution)/shard_map/all_to_all | solution.py:38
  46.2 2.1 reshape.129
  48.3 1.2 copy.42
  49.6 0.9 pad_maximum_fusion
  50.4 0.0 all-gather.2.cloned.1.call-update
  51.1 0.0 copy-start.9
  51.1 0.0 copy-start.10
  51.1 3.0 copy.43
  54.3 4.3 %fusion.19 = f32[5376,256]{1,0:T(8,128)} fusion(bf16[5376,256]{1,0:T(8,128)(2,1)S(1)} %copy-done.3, bf16[768,256]{1,0:T(8,128)(2,1)} %param.24), kind=kOutput, calls=%fused_computation.33 | convolution fusion | flops 704643072 | bytes 8388608 | tf_op jit(solution)/shard_map/dot_general | solution.py:48
  58.5 22.3 %all-gather.2.cloned.1.call-done = bf16[4608,256]{0,1:T(8,128)(2,1)} async-done(((bf16[4608,64]{0,1:T(8,128)(2,1)}), bf16[4608,256]{0,1:T(8,128)(2,1)}) %all-gather.2.cloned.1.call-update) | async-done | bytes 2359312 | tf_op jit(solution)/shard_map/all_gather | solution.py:42
  80.8 2.8 copy.44
  83.7 15.8 %gather_fusion.1 = bf16[5376,256]{1,0:T(8,128)(2,1)} fusion(bf16[4608,256]{1,0:T(8,128)(2,1)S(1)} %copy.44, s32[6144]{0:T(1024)S(1)} %pad_clamp_fusion.1), kind=kCustom, calls=%fused_computation.1 | custom fusion | bytes 5526528 | tf_op jit(solution)/shard_map/gather | solution.py:46
  99.5 15.8 %gather_fusion.2 = bf16[5376,256]{1,0:T(8,128)(2,1)} fusion(bf16[4608,256]{1,0:T(8,128)(2,1)S(1)} %copy.44, s32[6144]{0:T(1024)S(1)} %pad_clamp_fusion), kind=kCustom, calls=%fused_computation.2 | custom fusion | bytes 5526528 | tf_op jit(solution)/shard_map/gather | solution.py:47
  115.2 6.8 %convolution_add_fusion.2 = f32[5376,256]{1,0:T(8,128)} fusion(f32[5376,256]{1,0:T(8,128)} %fusion.19, bf16[5376,256]{1,0:T(8,128)(2,1)} %gather_fusion.1, bf16[768,256]{1,0:T(8,128)(2,1)} %param.24), kind=kOutput, calls=%fused_computation.8 | convolution fusion | flops 706019328 | bytes 13893632 | tf_op jit(solution)/shard_map/dot_general | solution.py:49
  122.1 8.1 %fusion.27 = (f32[5376]{0:T(1024)S(1)}, f32[5376,256]{0,1:T(8,128)}) fusion(f32[256]{0:T(256)S(1)} %copy-done.15, bf16[256,256]{1,0:T(8,128)(2,1)S(1)} %copy-done, f32[5376,256]{1,0:T(8,128)} %convolution_add_fusion.2, bf16[5376,256]{1,0:T(8,128)(2,1)} %gather_fusion.2, f32[256]{0:T(256)S(1)} %copy-done.16, bf16[768,256]{1,0:T(8,128)(2,1)} %param.24), kind=kOutput, calls=%fused_computation.51 | convolution fusion | flops 1421667072 | bytes 14048256 | tf_op jit(solution)/shard_map/dot_general | solution.py:56
  130.2 0.0 copy-start.12
  130.2 3.3 multiply_reduce_fusion
  133.5 0.8 copy-done.2
  134.4 5.2 %convert_multiply_fusion = (f32[5376,256]{0,1:T(8,128)}, bf16[5376,256]{0,1:T(8,128)(2,1)}) fusion(f32[5376]{0:T(1024)S(1)} %fusion.24, f32[256]{0:T(256)S(1)} %copy-done.11, f32[256]{0:T(256)S(1)} %copy-done.12, f32[5376]{0:T(1024)S(1)} %add_rsqrt_fusion, f32[5376,256]{0,1:T(8,128)S(1)} %copy-done.2, f32[5376]{0:T(1024)S(1)} %broadcast_multiply_fusion, ...), kind=kLoop, calls=%fused_computation.9 | loop fusion | flops 13762560 | bytes 16581632 | tf_op jit(solution)/shard_map/mul | solution.py:62
  139.6 6.1 %copy.46 = f32[5376,256]{1,0:T(8,128)} copy(f32[5376,256]{0,1:T(8,128)} %get-tuple-element.14) | data formatting | bytes 11010048 | tf_op jit(solution)/shard_map/mul | solution.py:62
  145.8 30.8 %scatter_custom_fusion = f32[4608,256]{1,0:T(8,128)} fusion(s32[5376]{0:T(1024)S(1)} %copy-done.10, f32[5376,256]{1,0:T(8,128)} %copy.46, f32[]{:T(128)} %constant.13.clone.1), kind=kCustom, calls=%fused_computation.15 | custom fusion | flops 1376256 | bytes 4719104 | tf_op jit(solution)/shard_map/scatter-add | solution.py:63
  176.6 2.7 slice.61
  179.3 12.6 %all-to-all-start.1 = ((bf16[64,32,256]{2,1,0:T(8,128)(2,1)}), bf16[64,32,256]{2,1,0:T(8,128)(2,1)}, u32[]{:S(2)}, u32[]{:S(2)}) async-start(bf16[64,32,256]{2,1,0:T(8,128)(2,1)} %bitcast.4), calls=%async_computation.1 | async-start | bytes 2097152 | tf_op jit(solution)/shard_map/all_to_all | solution.py:68
  191.9 0.0 slice-start
  191.9 0.0 reduce-scatter.2.cloned.1.call-start
  192.0 0.1 reshape.114
  192.1 28.1 %all-to-all-done.1 = bf16[64,32,256]{2,1,0:T(8,128)(2,1)} async-done(((bf16[64,32,256]{2,1,0:T(8,128)(2,1)}), bf16[64,32,256]{2,1,0:T(8,128)(2,1)}, u32[]{:S(2)}, u32[]{:S(2)}) %all-to-all-start.1) | async-done | bytes 1048608 | tf_op jit(solution)/shard_map/all_to_all | solution.py:68
  220.1 13.0 %scatter_custom_fusion.1 = f32[2560,256]{1,0:T(8,128)S(1)} fusion(f32[2560,256]{1,0:T(8,128)S(1)} %slice-done, s32[2048]{0:T(1024)S(1)} %reshape.114, bf16[2048,256]{1,0:T(8,128)(2,1)} %bitcast.6), kind=kCustom, calls=%fused_computation.18 | custom fusion | flops 1048576 | bytes 3670016 | tf_op jit(solution)/shard_map/scatter-add | solution.py:71
  233.1 0.0 copy-start.7
  233.1 0.0 copy-start.8
  233.1 51.9 %all-reduce.2 = bf16[2560,256]{1,0:T(8,128)(2,1)} all-reduce(f32[2560,256]{1,0:T(8,128)S(1)} %scatter_custom_fusion.1), channel_id=1, replica_groups=mesh['dom'=64,'chan'=4] {'chan'}, use_global_device_ids=true, to_apply=%region_4.0 | all-reduce | flops 655360 | bytes 3932160 | tf_op jit(solution)/shard_map/psum | solution.py:75
  285.1 2.7 fusion.7
  287.7 3.9 %fusion.12 = f32[2560,256]{0,1:T(8,128)} fusion(bf16[64,256]{1,0:T(8,128)(2,1)S(1)} %copy-done.8, f32[2560,64]{0,1:T(8,128)} %fusion.7, bf16[4608,256]{0,1:T(8,128)(2,1)} %all-gather.2.cloned.1.call-done, f32[64]{0:T(128)S(1)} %convert_element_type.47, bf16[512,64]{0,1:T(8,128)(2,1)S(1)} %copy-done.7), kind=kOutput, calls=%fused_computation.26 | convolution fusion | flops 168919040 | bytes 4653568 | tf_op jit(solution)/shard_map/dot_general | solution.py:80
  291.7 0.0 reduce-scatter.2.cloned.1.call-update
  291.7 0.1 dynamic_slice.3
  291.8 2.7 copy.48
  294.5 27.1 %reduce-scatter.2.cloned.1.call-done = f32[2560,64]{0,1:T(8,128)} async-done(((f32[2560,256]{0,1:T(8,128)}), f32[2560,64]{0,1:T(8,128)}) %reduce-scatter.2.cloned.1.call-update) | async-done | bytes 655376 | tf_op jit(solution)/shard_map/reduce_scatter | solution.py:81
  321.6 1.3 add_reduce_fusion
  322.8 10.3 %all-reduce = (f32[2560]{0:T(1024)S(1)}, f32[2560]{0:T(1024)S(1)}) all-reduce(f32[2560]{0:T(1024)S(1)} %get-tuple-element.11, f32[2560]{0:T(1024)S(1)} %get-tuple-element.10), channel_id=1, replica_groups=mesh['dom'=64,'chan'=4] {'chan'}, use_global_device_ids=true, to_apply=%region_9.0 | all-reduce | flops 5120 | bytes 40960 | tf_op jit(solution)/shard_map/psum | solution.py:83
  333.1 2.1 add_convert_fusion.1
  (42 shorter events, 0.1 us)
Async XLA Ops:
  7.2 114.9 %copy-start = (bf16[256,256]{1,0:T(8,128)(2,1)S(1)}, bf16[256,256]{1,0:T(8,128)(2,1)}, u32[]{:S(2)}) copy-start(bf16[256,256]{1,0:T(8,128)(2,1)} %param.26) | copy-start | bytes 393220
  7.2 73.7 %all-gather.2.cloned.1.call-start = ((), (), s32[]{:S(2)}) async-start(), calls=%async_computation.3 | async-start | bytes 2949120 | tf_op jit(solution)/shard_map/all_gather | solution.py:42
  9.5 40.1 %copy-start.6 = (bf16[2560,64]{0,1:T(8,128)(2,1)S(1)}, bf16[2560,64]{0,1:T(8,128)(2,1)}, u32[]{:S(2)}) copy-start(bf16[2560,64]{0,1:T(8,128)(2,1)} %param.18) | copy-start | bytes 983044
  17.5 33.6 %copy-start.3 = (bf16[5376,256]{1,0:T(8,128)(2,1)S(1)}, bf16[5376,256]{1,0:T(8,128)(2,1)}, u32[]{:S(2)}) copy-start(bf16[5376,256]{1,0:T(8,128)(2,1)} %param.19) | copy-start | bytes 8257540
  51.1 3.1 copy-start.9
  51.1 3.1 copy-start.10
  115.2 6.8 %copy-start.15 = (f32[256]{0:T(256)S(1)}, f32[256]{0:T(256)}, u32[]{:S(2)}) copy-start(f32[256]{0:T(256)} %param.27) | copy-start | bytes 3076
  115.2 6.8 %copy-start.16 = (f32[256]{0:T(256)S(1)}, f32[256]{0:T(256)}, u32[]{:S(2)}) copy-start(f32[256]{0:T(256)} %param.25) | copy-start | bytes 3076
  122.1 11.4 %copy-start.5 = (bf16[5376,256]{0,1:T(8,128)(2,1)S(1)}, bf16[5376,256]{0,1:T(8,128)(2,1)}, u32[]{:S(2)}) copy-start(bf16[5376,256]{0,1:T(8,128)(2,1)} %copy.43) | copy-start | bytes 8257540
  130.2 4.2 %copy-start.2 = (f32[5376,256]{0,1:T(8,128)S(1)}, f32[5376,256]{0,1:T(8,128)}, u32[]{:S(2)}) copy-start(f32[5376,256]{0,1:T(8,128)} %get-tuple-element.19) | copy-start | bytes 16515076
  130.2 4.2 %copy-start.11 = (f32[256]{0:T(256)S(1)}, f32[256]{0:T(256)}, u32[]{:S(2)}) copy-start(f32[256]{0:T(256)} %param.29) | copy-start | bytes 3076
  130.2 4.2 %copy-start.12 = (f32[256]{0:T(256)S(1)}, f32[256]{0:T(256)}, u32[]{:S(2)}) copy-start(f32[256]{0:T(256)} %param.28) | copy-start | bytes 3076
  176.6 15.5 %copy-start.18 = (bf16[64]{0:T(256)(128)(2,1)S(1)}, bf16[64]{0:T(256)(128)(2,1)}, u32[]{:S(2)}) copy-start(bf16[64]{0:T(256)(128)(2,1)} %param.31) | copy-start | bytes 388
  179.3 40.8 %all-to-all-start.1 = ((bf16[64,32,256]{2,1,0:T(8,128)(2,1)}), bf16[64,32,256]{2,1,0:T(8,128)(2,1)}, u32[]{:S(2)}, u32[]{:S(2)}) async-start(bf16[64,32,256]{2,1,0:T(8,128)(2,1)} %bitcast.4), calls=%async_computation.1 | async-start | bytes 2097152 | tf_op jit(solution)/shard_map/all_to_all | solution.py:68
  191.9 28.2 %slice-start = ((f32[4608,256]{1,0:T(8,128)}), f32[2560,256]{1,0:T(8,128)S(1)}, s32[]{:S(2)}) async-start(f32[4608,256]{1,0:T(8,128)} %scatter_custom_fusion), calls=%async_computation.5 | async-start | bytes 5242880 | tf_op jit(solution)/shard_map/slice | solution.py:66
  191.9 129.6 %reduce-scatter.2.cloned.1.call-start = ((), (), s32[]{:S(2)}) async-start(), calls=%async_computation.4 | async-start | bytes 3276800 | tf_op jit(solution)/shard_map/reduce_scatter | solution.py:81
  233.1 51.9 %copy-start.7 = (bf16[512,64]{0,1:T(8,128)(2,1)S(1)}, bf16[512,64]{0,1:T(8,128)(2,1)}, u32[]{:S(2)}) copy-start(bf16[512,64]{0,1:T(8,128)(2,1)} %param.30) | copy-start | bytes 196612
  233.1 54.6 %copy-start.8 = (bf16[64,256]{1,0:T(8,128)(2,1)S(1)}, bf16[64,256]{1,0:T(8,128)(2,1)}, u32[]{:S(2)}) copy-start(bf16[64,256]{1,0:T(8,128)(2,1)} %param.32) | copy-start | bytes 98308
  287.7 4.0 %copy-start.17 = (f32[256]{0:T(256)S(1)}, f32[256]{0:T(256)}, u32[]{:S(2)}) copy-start(f32[256]{0:T(256)} %param.33) | copy-start | bytes 3076
  287.7 4.0 %copy-start.4 = (bf16[5376,256]{0,1:T(8,128)(2,1)S(1)}, bf16[5376,256]{0,1:T(8,128)(2,1)}, u32[]{:S(2)}) copy-start(bf16[5376,256]{0,1:T(8,128)(2,1)} %get-tuple-element.15) | copy-start | bytes 8257540
  291.8 43.4 %copy-start.1 = (bf16[256,256]{1,0:T(8,128)(2,1)S(1)}, bf16[256,256]{1,0:T(8,128)(2,1)}, u32[]{:S(2)}) copy-start(bf16[256,256]{1,0:T(8,128)(2,1)} %param.26) | copy-start | bytes 393220
  291.8 41.3 %copy-start.13 = (f32[64]{0:T(128)S(1)}, f32[64]{0:T(128)}, u32[]{:S(2)}) copy-start(f32[64]{0:T(128)} %param.35) | copy-start | bytes 772
  291.8 41.3 %copy-start.14 = (f32[64]{0:T(128)S(1)}, f32[64]{0:T(128)}, u32[]{:S(2)}) copy-start(f32[64]{0:T(128)} %param.34) | copy-start | bytes 772
Sparse Core Ops, SparseCore 0:
  50.6 30.2 all-gather.1
  291.8 29.6 reduce-scatter.1
where the time goes:
time: 343 us; the launch traced here: 342 us
  blocking collectives  89.3 us (26%)
  waiting for transfers between devices  77.5 us (23%)
  local copies, waits for them, and re-layouts  65.2 us (19%)
  other arithmetic  56.6 us (17%)
  matrix products  25.8 us (8%)
  between operations  15 us (4%)
  starting transfers between devices  12.7 us (4%)
    psum x1, blocking collectives, body(): summed = lax.psum(local_part, 'chan')  51.9 us
    scatter-add x1, other arithmetic, body(): jax.ops.segment_sum(messages, receivers, num_segments=node_rows + part_co...  30.8 us
    all_to_all x1, waiting for transfers between devices, body(): lax.all_to_all(halo_part.astype(jnp.bfloat16), 'dom', split_axis=0, conca...  28.1 us
    all_to_all x1, blocking collectives, body(): lax.all_to_all(outgoing, 'dom', split_axis=0, concat_axis=0, tiled=True)  27.2 us
    reduce_scatter x1, waiting for transfers between devices, body(): lax.psum_scatter(node_terms, 'chan', scatter_dimension=1, tiled=True)  27.1 us
    all_gather x1, waiting for transfers between devices, body(): table = lax.all_gather(table, 'chan', axis=1, tiled=True)  22.3 us
    gather x1, local copies, waits for them, and re-layouts, body(): sender_feats = table[senders]  15.8 us
    gather x1, local copies, waits for them, and re-layouts, body(): receiver_feats = table[receivers]  15.8 us
  transfers between devices with their start and end apart: 3, of which 3 were waited for; matrix products, arithmetic and copies ran while one was open for 3% of the time, Pallas kernels for 0%

commit v1 on v0

v1 whole, which is shorter than its diff:
```python
import functools

import jax
import jax.numpy as jnp
from jax import lax
from jax.experimental import pallas as pl
from jax.experimental.pallas import tpu as pltpu
from jax.sharding import PartitionSpec as P

LANES = 128
EDGE_TILE = 768
UNROLL = 16
COPIES = 4
CHUNK = 512


def silu_rows(values):
    return values * jax.nn.sigmoid(values)


def edge_kernel(
    senders, receivers, live, own_rows, edges, w_in, b_in, w_out, b_out, gain, shift,
    edge_new, sums, sent, received, gathered, messages, *partial,
):
    step = pl.program_id(0)
    tile, latent = edges.shape

    def project(weights, target, rows):
        def chunk(k, carry):
            start = pl.multiple_of(k * CHUNK, CHUNK)
            block = jnp.dot(
                own_rows[pl.ds(start, CHUNK), :], weights, preferred_element_type=jnp.float32
            )
            target[pl.ds(2 * start, CHUNK, stride=2), :] = block[:, :LANES]
            target[pl.ds(2 * start + 1, CHUNK, stride=2), :] = block[:, LANES:]
            return carry

        lax.fori_loop(0, rows // CHUNK, chunk, 0)

    @pl.when(step == 0)
    def _():
        project(w_in[latent : 2 * latent, :], sent, sent.shape[0] // 2)
        project(w_in[2 * latent :, :], received, received.shape[0] // 2)
        for part in partial:
            part[...] = jnp.zeros_like(part)

    base = step * tile

    def gather(k, carry):
        for u in range(UNROLL):
            j = k * UNROLL + u
            s = senders[base + j]
            r = receivers[base + j]
            gathered[pl.ds(2 * j, 2), :] = sent[pl.ds(2 * s, 2), :] + received[pl.ds(2 * r, 2), :]
        return carry

    lax.fori_loop(0, tile // UNROLL, gather, 0)

    latents = edges[...]
    pre = jnp.dot(latents, w_in[:latent, :], preferred_element_type=jnp.float32)
    low = pre[:, :LANES] + gathered[pl.ds(0, tile, stride=2), :]
    high = pre[:, LANES:] + gathered[pl.ds(1, tile, stride=2), :]
    hidden = silu_rows(jnp.concatenate([low, high], axis=1) + b_in[...]).astype(jnp.bfloat16)
    post = jnp.dot(hidden, w_out[...], preferred_element_type=jnp.float32) + b_out[...]
    centred = post - jnp.mean(post, axis=-1, keepdims=True)
    var = jnp.mean(centred * centred, axis=-1, keepdims=True)
    norm = centred * lax.rsqrt(var + 1e-05) * gain[...] + shift[...]
    row = lax.broadcasted_iota(jnp.int32, (tile, 1), 0) + base
    norm = jnp.where(row < live[0], norm, 0.0)
    new = (latents.astype(jnp.float32) + norm).astype(jnp.bfloat16)
    edge_new[...] = new
    wide = new.astype(jnp.float32)
    messages[pl.ds(0, tile, stride=2), :] = wide[:, :LANES]
    messages[pl.ds(1, tile, stride=2), :] = wide[:, LANES:]

    def add_row(j, part):
        rows = pl.ds(2 * receivers[base + j], 2)
        part[rows, :] = part[rows, :] + messages[pl.ds(2 * j, 2), :]

    def scatter(k, carry):
        for u in range(UNROLL):
            add_row(k * UNROLL + u, partial[u % COPIES])
        return carry

    def scatter_one(j, carry):
        add_row(j, partial[0])
        return carry

    count = jnp.clip(live[0] - base, 0, tile)
    whole = count // UNROLL
    lax.fori_loop(0, whole, scatter, 0)
    lax.fori_loop(whole * UNROLL, count, scatter_one, 0)

    @pl.when(step == pl.num_programs(0) - 1)
    def _():
        def chunk(k, carry):
            start = pl.multiple_of(k * CHUNK, CHUNK)
            low = partial[0][pl.ds(2 * start, CHUNK, stride=2), :]
            high = partial[0][pl.ds(2 * start + 1, CHUNK, stride=2), :]
            for part in partial[1:]:
                low += part[pl.ds(2 * start, CHUNK, stride=2), :]
                high += part[pl.ds(2 * start + 1, CHUNK, stride=2), :]
            sums[pl.ds(start, CHUNK), :] = jnp.concatenate([low, high], axis=1).astype(sums.dtype)
            return carry

        lax.fori_loop(0, sums.shape[0] // CHUNK, chunk, 0)


def edge_block(node_rows, senders, receivers, live, table, edges, w_in, b_in, w_out, b_out, gain, shift):
    edge_rows, latent = edges.shape
    table_rows = table.shape[0]
    tile = EDGE_TILE
    full = lambda array: pl.BlockSpec(array.shape, lambda i, *_: (0, 0))
    tiled = pl.BlockSpec((tile, latent), lambda i, *_: (i, 0))
    scratch = lambda rows: pltpu.VMEM((2 * rows, LANES), jnp.float32)
    b_in, b_out, gain, shift = (v.reshape(1, latent) for v in (b_in, b_out, gain, shift))
    return pl.pallas_call(
        edge_kernel,
        grid_spec=pltpu.PrefetchScalarGridSpec(
            num_scalar_prefetch=3,
            grid=(edge_rows // tile,),
            in_specs=[full(table), tiled, full(w_in), full(b_in), full(w_out)] + [full(b_in)] * 3,
            out_specs=[tiled, pl.BlockSpec((table_rows, latent), lambda i, *_: (0, 0))],
            scratch_shapes=[scratch(node_rows), scratch(table_rows), scratch(tile), scratch(tile)]
            + [scratch(table_rows)] * COPIES,
        ),
        out_shape=[
            jax.ShapeDtypeStruct((edge_rows, latent), jnp.bfloat16),
            jax.ShapeDtypeStruct((table_rows, latent), jnp.bfloat16),
        ],
        compiler_params=pltpu.CompilerParams(vmem_limit_bytes=54 * 2**20),
        name="edges",
    )(senders, receivers, live, table, edges, w_in, b_in, w_out, b_out, gain, shift)


def body(
    node_latent,
    edge_latent,
    senders,
    receivers,
    edge_count,
    send_list,
    w_edge_in,
    edge_in_bias,
    w_edge_out,
    edge_out_bias,
    edge_gain,
    edge_shift,
    w_node_in,
    node_in_bias,
    w_node_out,
    node_out_bias,
    node_gain,
    node_shift,
):
    node_rows, quarter = node_latent.shape
    latent = w_edge_out.shape[0]
    part_count = lax.axis_size("dom")
    chan_size = lax.axis_size("chan")
    send_rows = send_list[0]
    slot_count = send_rows.shape[1]
    chan_index = lax.axis_index("chan")
    node_weights = lax.all_gather(
        jnp.concatenate([w_node_in.T, w_node_out], axis=1), "chan", axis=0, tiled=True
    )
    node_vectors = lax.all_gather(
        jnp.stack([node_in_bias.astype(jnp.float32), node_gain, node_shift]), "chan", axis=1, tiled=True
    )
    outgoing = node_latent[send_rows.reshape(-1)].reshape(part_count, slot_count, quarter)
    incoming = lax.all_to_all(outgoing, "dom", split_axis=0, concat_axis=0, tiled=True)
    table = jnp.concatenate(
        [node_latent, incoming.reshape(part_count * slot_count, quarter)], axis=0
    )
    table = lax.all_gather(table, "chan", axis=1, tiled=True)
    edge_rows = edge_latent.shape[0]
    live = jnp.clip(edge_count - chan_index * edge_rows, 0, edge_rows)
    edge_new, sums = edge_block(
        node_rows, senders, receivers, live, table, edge_latent, w_edge_in, edge_in_bias, w_edge_out,
        edge_out_bias, edge_gain, edge_shift,
    )
    halo = lax.psum_scatter(
        sums[node_rows:].reshape(part_count, slot_count, latent), "chan", scatter_dimension=1, tiled=True
    )
    returned = lax.all_to_all(halo, "dom", split_axis=0, concat_axis=0, tiled=True)
    slots = slot_count // chan_size
    my_rows = lax.dynamic_slice_in_dim(send_rows, chan_index * slots, slots, 1)
    local = sums[:node_rows].astype(jnp.float32) + jax.ops.segment_sum(
        returned.astype(jnp.float32).reshape(-1, latent), my_rows.reshape(-1), num_segments=node_rows
    )
    own = node_rows // chan_size
    summed = lax.psum_scatter(local, "chan", scatter_dimension=0, tiled=True).astype(jnp.bfloat16)
    nodes = lax.dynamic_slice_in_dim(table, chan_index * own, own, 0)
    across = (((1,), (1,)), ((), ()))
    pre = lax.dot_general(
        nodes, node_weights[:, :latent], across, preferred_element_type=jnp.float32
    ) + lax.dot_general(
        summed, node_weights[:, latent : 2 * latent], across, preferred_element_type=jnp.float32
    )
    hidden = silu_rows(pre + node_vectors[0]).astype(jnp.bfloat16)
    post = (
        jnp.dot(hidden, node_weights[:, 2 * latent :], preferred_element_type=jnp.float32) + node_out_bias
    )
    centred = post - jnp.mean(post, axis=-1, keepdims=True)
    var = jnp.mean(centred * centred, axis=-1, keepdims=True)
    norm = centred * lax.rsqrt(var + 1e-05) * node_vectors[1] + node_vectors[2]
    new = (nodes.astype(jnp.float32) + norm).astype(jnp.bfloat16)
    node_new = lax.all_to_all(new, "chan", split_axis=1, concat_axis=0, tiled=True)
    return (node_new, edge_new)


def solution(mesh):
    placed = (
        P("dom", "chan"),
        P(("dom", "chan"), None),
        P(("dom", "chan")),
        P(("dom", "chan")),
        P("dom"),
        P("dom", None, None),
        P(),
        P(),
        P(),
        P(),
        P(),
        P(),
        P(None, "chan"),
        P("chan"),
        P("chan", None),
        P(),
        P("chan"),
        P("chan"),
    )
    return jax.shard_map(
        body,
        mesh=mesh,
        in_specs=placed,
        out_specs=(P("dom", "chan"), P(("dom", "chan"), None)),
        check_vma=False,
    )
```

time: 343 us -> 229 us (0.67)
  other arithmetic: 56.6 us -> 7.99 us
  local copies, waits for them, and re-layouts: 65.2 us -> 20.9 us
  Pallas kernels: 0 us -> 38.6 us
  blocking collectives: 89.3 us -> 52.7 us
  matrix products: 25.8 us -> 2.94 us
    psum x2 -> x0, blocking collectives: 62.2 us -> none  [the longest x1 51.9 us: body(): summed = lax.psum(local_part, 'chan')]
    scatter-add x2 -> x1, other arithmetic: 43.8 us -> 4.3 us  [body(): jax.ops.segment_sum(returned.astype(jnp.float32).reshape(-1, latent), my_...]
    pallas_call x0 -> x1, Pallas kernels: none -> 38.6 us  [edge_block(): pl.pallas_call(edge_kernel, grid_spec=pltpu.PrefetchScalarGridSpec(num_sc...]
    gather x2 -> x0, local copies, waits for them, and re-layouts: 31.6 us -> none  [the longest x1 15.8 us: body(): sender_feats = table[senders]]
    unnamed x2 -> x4, waiting for transfers between devices: 0.03 us -> 22.9 us
    dot_general x5 -> x2, matrix products: 25.8 us -> 2.94 us  [the longest x1 1.67 us: body(): jnp.dot(hidden, node_weights[:, 2 * latent:], preferred_element_type=jnp....]
    all_to_all x1, waiting for transfers between devices: 28.1 us -> 11 us  [body(): lax.all_to_all(halo, 'dom', split_axis=0, concat_axis=0, tiled=True)]
    all_gather x0 -> x2, blocking collectives: none -> 16.9 us  [the longest x1 9.09 us: body(): lax.all_gather(jnp.concatenate([w_node_in.T, w_node_out], axis=1), 'chan'...]
  transfers between devices with their start and end apart: 3 -> 4, of which waited for: 3 -> 4; matrix products, arithmetic and copies ran while one was open for 3% -> 2% of each run, Pallas kernels for 0% -> 0%
where the time goes in v1:
time: 229 us
  waiting for transfers between devices  78.3 us (34%)
  blocking collectives  52.7 us (23%)
  Pallas kernels  38.6 us (17%)
  local copies, waits for them, and re-layouts  20.9 us (9%)
  between operations  14.6 us (6%)
  starting transfers between devices  12.5 us (5%)
  other arithmetic  7.99 us (3%)
  matrix products  2.94 us (1%)
    pallas_call x1, Pallas kernels, edge_block(): pl.pallas_call(edge_kernel, grid_spec=pltpu.PrefetchScalarGridSpec(num_sc...  38.6 us
    all_gather x1, waiting for transfers between devices, body(): table = lax.all_gather(table, 'chan', axis=1, tiled=True)  29.7 us
    all_to_all x1, blocking collectives, body(): lax.all_to_all(outgoing, 'dom', split_axis=0, concat_axis=0, tiled=True)  27 us
    unnamed x4, waiting for transfers between devices  22.9 us
    reduce_scatter x1, waiting for transfers between devices, body(): lax.psum_scatter(local, 'chan', scatter_dimension=0, tiled=True)  14.7 us
    all_to_all x1, starting transfers between devices, body(): lax.all_to_all(halo, 'dom', split_axis=0, concat_axis=0, tiled=True)  12.4 us
    all_to_all x1, waiting for transfers between devices, body(): lax.all_to_all(halo, 'dom', split_axis=0, concat_axis=0, tiled=True)  11 us
    all_gather x1, blocking collectives, body(): lax.all_gather(jnp.concatenate([w_node_in.T, w_node_out], axis=1), 'chan'...  9.09 us
  transfers between devices with their start and end apart: 4, of which 4 were waited for; matrix products, arithmetic and copies ran while one was open for 2% of the time, Pallas kernels for 0%

profile of v1, /device:TPU:1, one launch (start us, length us, event | category | flops | bytes accessed | tf_op | source)
XLA Modules:
  0.0 228.6 jit_solution(6535317262899501240)
XLA Ops:
  7.2 0.0 all-gather.3.cloned.1.call-start
  7.2 1.3 copy.47
  8.5 0.8 copy.46
  9.3 0.1 reshape_squeeze.3
  9.4 6.2 %gather_fusion = bf16[2048,64]{1,0:T(8,128)(2,1)S(1)} fusion(bf16[2560,64]{1,0:T(8,128)(2,1)S(1)} %copy.47, s32[2048]{0:T(1024)S(1)} %broadcast_clamp_fusion), kind=kCustom, calls=%fused_computation | custom fusion | bytes 532480 | tf_op jit(solution)/shard_map/gather | solution.py:169
  15.6 0.0 copy-start.1
  15.6 0.3 reshape.112
  15.9 27.0 %all_to_all.29 = bf16[64,2,1024]{2,1,0:T(2,128)(2,1)S(1)} all-to-all(bf16[64,2,1024]{2,1,0:T(2,128)(2,1)S(1)} %reshape.112), channel_id=1, replica_groups=mesh['dom'=64,'chan'=4] {'dom'}, dimensions={0} | all-to-all | bytes 524288 | tf_op jit(solution)/shard_map/all_to_all | solution.py:170
  43.0 0.3 reshape.113
  43.3 0.2 copy.48
  43.6 0.9 pad_maximum_fusion
  44.4 0.0 all-gather.3.cloned.1.call-update
  44.4 0.0 reduce-scatter.7.cloned.1.call-start
  45.1 29.7 %all-gather.3.cloned.1.call-done = bf16[4608,256]{0,1:T(8,128)(2,1)} async-done(((bf16[4608,64]{0,1:T(8,128)(2,1)}), bf16[4608,256]{0,1:T(8,128)(2,1)}) %all-gather.3.cloned.1.call-update) | async-done | bytes 2359312 | tf_op jit(solution)/shard_map/all_gather | solution.py:174
  74.8 4.3 %copy.49.own_rows = bf16[4608,256]{1,0:T(8,128)(2,1)} copy(bf16[4608,256]{0,1:T(8,128)(2,1)} %all-gather.3.cloned.1.call-done) | data formatting | bytes 4718592 | tf_op jit(solution)/shard_map/all_gather | solution.py:174
  79.1 38.6 %edges.2 = (bf16[5376,256]{1,0:T(8,128)(2,1)}, bf16[4608,256]{1,0:T(8,128)(2,1)}) custom-call(s32[5376]{0:T(1024)} %senders.1, s32[5376]{0:T(1024)} %receivers.1, s32[1]{0:T(128)S(6)} %min.6.live, bf16[4608,256]{1,0:T(8,128)(2,1)} %copy.49.own_rows, bf16[5376,256]{1,0:T(8,128)(2,1)} %edges.3, bf16[768,256]{1,0:T(8,128)(2,1)} %w_in.1, f32[1,256]{1,0:T(1,128)} %bitcast.61, ...), custom_call_target="tpu_custom_call" | custom-call | tf_op jit(solution)/shard_map/edges/pallas_call | solution.py:117
  117.6 1.3 slice.26
  118.9 1.1 copy.56
  120.0 0.0 reduce-scatter.7.cloned.1.call-update
  120.1 0.7 constant_dynamic-slice_fusion
  120.7 0.1 copy.50
  120.8 0.1 reshape.99
  120.9 22.9 %reduce-scatter.7.cloned.1.call-done = bf16[8,16384]{1,0:T(8,128)(2,1)} async-done(((bf16[32,16384]{1,0:T(8,128)(2,1)}), bf16[8,16384]{1,0:T(8,128)(2,1)}) %reduce-scatter.7.cloned.1.call-update) | async-done | bytes 262160
  143.8 1.0 copy.60
  144.8 0.9 copy.54
  145.7 12.4 %all-to-all-start.1 = ((bf16[64,8,256]{2,1,0:T(8,128)(2,1)}), bf16[64,8,256]{2,1,0:T(8,128)(2,1)S(1)}, u32[]{:S(2)}, u32[]{:S(2)}) async-start(bf16[64,8,256]{2,1,0:T(8,128)(2,1)} %copy.54), calls=%async_computation.1 | async-start | bytes 524288 | tf_op jit(solution)/shard_map/all_to_all | solution.py:184
  158.0 0.0 reduce-scatter.5.cloned.1.call-start
  158.1 1.5 slice_convert_fusion
  159.6 0.0 copy-start.7
  159.6 0.0 copy-start.4
  159.6 0.0 copy-start.5
  159.6 0.0 copy-start.2
  159.7 0.0 copy-start.3
  159.7 11.0 %all-to-all-done.1 = bf16[64,8,256]{2,1,0:T(8,128)(2,1)S(1)} async-done(((bf16[64,8,256]{2,1,0:T(8,128)(2,1)}), bf16[64,8,256]{2,1,0:T(8,128)(2,1)S(1)}, u32[]{:S(2)}, u32[]{:S(2)}) %all-to-all-start.1) | async-done | bytes 262176 | tf_op jit(solution)/shard_map/all_to_all | solution.py:184
  170.6 4.3 %scatter_custom_fusion = f32[2560,256]{1,0:T(8,128)S(1)} fusion(f32[2560,256]{1,0:T(8,128)S(1)} %slice_convert_fusion, s32[512]{0:T(512)S(1)} %reshape.99, bf16[64,8,256]{2,1,0:T(8,128)(2,1)S(1)} %all-to-all-done.1), kind=kCustom, calls=%fused_computation.10 | custom fusion | flops 262144 | bytes 2883584 | tf_op jit(solution)/shard_map/scatter-add | solution.py:187
  174.9 0.0 copy-start.6
  175.0 1.5 copy-done
  176.5 0.0 reduce-scatter.5.cloned.1.call-update
  176.5 7.8 %all-gather = f32[4,64,3]{1,2,0:T(4,128)S(1)} all-gather(f32[1,64,3]{1,2,0:T(4,128)S(1)} %maximum_bitcast_fusion), channel_id=1, replica_groups=mesh['dom'=64,'chan'=4] {'chan'}, dimensions={0}, use_global_device_ids=true | all-gather | bytes 3840 | tf_op jit(solution)/shard_map/all_gather | solution.py:166
  184.4 0.1 reshape.107
  184.5 9.1 %all_gather.10 = bf16[256,768]{1,0:T(8,128)(2,1)S(1)} all-gather(bf16[64,768]{1,0:T(8,128)(2,1)S(1)} %pad_maximum_fusion.1), channel_id=1, replica_groups=mesh['dom'=64,'chan'=4] {'chan'}, dimensions={0}, use_global_device_ids=true | all-gather | bytes 491520 | tf_op jit(solution)/shard_map/all_gather | solution.py:163
  193.6 1.3 fusion.7
  194.8 14.7 %reduce-scatter.5.cloned.1.call-done = f32[640,256]{1,0:T(8,128)} async-done(((f32[2560,256]{1,0:T(8,128)}), f32[640,256]{1,0:T(8,128)}) %reduce-scatter.5.cloned.1.call-update) | async-done | bytes 655376 | tf_op jit(solution)/shard_map/reduce_scatter | solution.py:191
  209.6 1.7 fusion.17
  211.2 0.1 multiply_reduce_fusion
  211.4 1.2 add_convert_fusion
  212.5 8.8 %all_to_all.30 = bf16[640,4,64]{0,2,1:T(8,128)(2,1)S(1)} all-to-all(bf16[640,4,64]{0,2,1:T(8,128)(2,1)S(1)} %bitcast.52), channel_id=1, replica_groups=mesh['dom'=64,'chan'=4] {'chan'}, dimensions={1} | all-to-all | bytes 655360 | tf_op jit(solution)/shard_map/all_to_all | solution.py:207
  221.3 0.8 copy.55
  (17 shorter events, 0.1 us)
Async XLA Ops:
  7.2 67.7 %all-gather.3.cloned.1.call-start = ((), (), s32[]{:S(2)}) async-start(), calls=%async_computation.5 | async-start | bytes 2949120 | tf_op jit(solution)/shard_map/all_gather | solution.py:174
  15.6 27.9 %copy-start.1 = (bf16[2560,64]{0,1:T(8,128)(2,1)S(1)}, bf16[2560,64]{0,1:T(8,128)(2,1)}, u32[]{:S(2)}) copy-start(bf16[2560,64]{0,1:T(8,128)(2,1)} %param.18) | copy-start | bytes 983044
  44.4 99.4 %reduce-scatter.7.cloned.1.call-start = ((), (), s32[]{:S(2)}) async-start(), calls=%async_computation.7 | async-start | bytes 1310720
  145.7 25.0 %all-to-all-start.1 = ((bf16[64,8,256]{2,1,0:T(8,128)(2,1)}), bf16[64,8,256]{2,1,0:T(8,128)(2,1)S(1)}, u32[]{:S(2)}, u32[]{:S(2)}) async-start(bf16[64,8,256]{2,1,0:T(8,128)(2,1)} %copy.54), calls=%async_computation.1 | async-start | bytes 524288 | tf_op jit(solution)/shard_map/all_to_all | solution.py:184
  158.0 51.5 %reduce-scatter.5.cloned.1.call-start = ((), (), s32[]{:S(2)}) async-start(), calls=%async_computation.6 | async-start | bytes 3276800 | tf_op jit(solution)/shard_map/reduce_scatter | solution.py:191
  159.6 16.9 %copy-start.7 = (bf16[64]{0:T(256)(128)(2,1)S(1)}, bf16[64]{0:T(256)(128)(2,1)}, u32[]{:S(2)}) copy-start(bf16[64]{0:T(256)(128)(2,1)} %param.31) | copy-start | bytes 388
  159.6 16.9 %copy-start.4 = (f32[64]{0:T(128)S(1)}, f32[64]{0:T(128)}, u32[]{:S(2)}) copy-start(f32[64]{0:T(128)} %param.35) | copy-start | bytes 772
  159.6 16.9 %copy-start.5 = (f32[64]{0:T(128)S(1)}, f32[64]{0:T(128)}, u32[]{:S(2)}) copy-start(f32[64]{0:T(128)} %param.34) | copy-start | bytes 772
  159.6 24.8 %copy-start.2 = (bf16[512,64]{0,1:T(8,128)(2,1)S(1)}, bf16[512,64]{0,1:T(8,128)(2,1)}, u32[]{:S(2)}) copy-start(bf16[512,64]{0,1:T(8,128)(2,1)} %param.30) | copy-start | bytes 196612
  159.7 24.8 %copy-start.3 = (bf16[64,256]{1,0:T(8,128)(2,1)S(1)}, bf16[64,256]{1,0:T(8,128)(2,1)}, u32[]{:S(2)}) copy-start(bf16[64,256]{1,0:T(8,128)(2,1)} %param.32) | copy-start | bytes 98308
  174.9 1.5 copy-start
  174.9 34.6 %copy-start.6 = (f32[256]{0:T(256)S(1)}, f32[256]{0:T(256)}, u32[]{:S(2)}) copy-start(f32[256]{0:T(256)} %param.33) | copy-start | bytes 3076
Sparse Core Ops, SparseCore 0:
  44.6 30.2 all-gather.2
  120.2 23.6 reduce-scatter.6
  176.6 32.9 reduce-scatter.4

commit v2 on v1

v2 whole, which is shorter than its diff:
```python
import functools

import jax
import jax.numpy as jnp
from jax import lax
from jax.experimental import pallas as pl
from jax.experimental.pallas import tpu as pltpu
from jax.sharding import PartitionSpec as P

LANES = 128
EDGE_TILE = 768
UNROLL = 16
COPIES = 4
CHUNK = 512
GROUPS = 4
MESH = pl.DeviceIdType.MESH
FLOAT = jnp.float32
HALF = jnp.bfloat16
ANY = pl.BlockSpec(memory_space=pl.ANY)
VMEM = pl.BlockSpec(memory_space=pltpu.VMEM)


def silu_rows(values):
    return values * jax.nn.sigmoid(values)


def enter(dom, chan, parts, chans):
    barrier = pltpu.get_barrier_semaphore()

    def greet(k, carry):
        pl.semaphore_signal(barrier, inc=1, device_id=(lax.rem(dom + k, parts), chan), device_id_type=MESH)
        return carry

    lax.fori_loop(1, parts, greet, 0)
    for k in range(1, chans):
        pl.semaphore_signal(barrier, inc=1, device_id=(dom, lax.rem(chan + k, chans)), device_id_type=MESH)
    pl.semaphore_wait(barrier, parts + chans - 2)


def forward_kernel(
    send_rows, nodes, w_in, w_out, vectors,
    own, halo, all_in, all_out, all_vectors,
    wide, stage, outgoing, part_send, part_recv, send, recv, local,
    *, parts, chans,
):
    dom = lax.axis_index("dom")
    chan = lax.axis_index("chan")
    quarter, node_rows = nodes.shape
    slots = send_rows.shape[0] // 2
    sibling = (dom, chan + 1 - 2 * lax.rem(chan, 2))
    across = (dom, lax.rem(chan + 2, chans))
    far = lax.rem(chan + 2, chans)
    enter(dom, chan, parts, chans)

    def block(array, index):
        rows = array.shape[0] // chans
        return array.at[pl.ds(pl.multiple_of(index * rows, rows), rows), :]

    def push(src, dst, index, target):
        copy = pltpu.make_async_remote_copy(
            src_ref=src, dst_ref=dst, send_sem=send.at[index], recv_sem=recv.at[index],
            device_id=target, device_id_type=MESH,
        )
        copy.start()
        return copy

    gathered = [(nodes, own), (w_in, all_in), (w_out, all_out), (vectors, all_vectors)]
    near, wait_later, kept = [], [], []
    for index, (src, dst) in enumerate(gathered):
        near.append(push(src, block(dst, chan), 3 * index, across))
        wait_later.append(push(src, block(dst, chan), 3 * index + 1, sibling))
        keep = pltpu.make_async_copy(src, block(dst, chan), local.at[index])
        keep.start()
        kept.append(keep)

    for start in range(0, node_rows, LANES):
        piece = nodes[:, start : start + LANES].astype(FLOAT)
        wide[pl.ds(start, LANES), :] = jnp.concatenate([piece, piece], axis=0).T

    lane = lax.broadcasted_iota(jnp.int32, (1, LANES), 1)
    left = lane < quarter

    def fill(k):
        peer = lax.rem(dom + k + 1, parts)
        base = pl.multiple_of(k * slots, slots)
        for j in range(slots):
            low = wide[pl.ds(send_rows[j, peer], 1), :]
            high = wide[pl.ds(send_rows[j + slots, peer], 1), :]
            stage[pl.ds(base + j, 1), :] = jnp.where(left, low, high)
        outgoing[k] = stage[pl.ds(base, slots), :].astype(HALF)
        return peer, base

    group = parts // GROUPS

    def send_part(k, carry):
        peer, base = fill(k)
        pltpu.make_async_remote_copy(
            src_ref=outgoing.at[k], dst_ref=halo.at[chan, pl.ds(base, slots), :],
            send_sem=part_send, recv_sem=part_recv.at[k // group],
            device_id=(peer, chan), device_id_type=MESH,
        ).start()
        return carry

    lax.fori_loop(0, parts - 1, send_part, 0)
    _, base = fill(parts - 1)
    mine = pltpu.make_async_copy(
        outgoing.at[parts - 1], halo.at[chan, pl.ds(base, slots), :], part_recv.at[GROUPS - 1]
    )
    mine.start()

    relays = []
    for index, (src, dst) in enumerate(gathered):
        near[index].wait_recv()
        relays.append(push(block(dst, far), block(dst, far), 3 * index + 2, sibling))

    first = 3 * len(gathered)
    pieces = []
    for g in range(GROUPS):
        rows = pl.ds(g * group * slots, group * slots)
        piece = halo.at[chan, rows, :]
        pltpu.make_async_copy(piece, piece, part_recv.at[g]).wait()
        cross = push(piece, piece, first + 3 * g, across)
        wait_later.append(push(piece, piece, first + 3 * g + 1, sibling))
        pieces.append((rows, cross))
    for g, (rows, cross) in enumerate(pieces):
        cross.wait_recv()
        piece = halo.at[far, rows, :]
        relays.append(push(piece, piece, first + 3 * g + 2, sibling))
    for copy in wait_later + relays:
        copy.wait()
    for copy in near + [cross for _, cross in pieces]:
        copy.wait_send()
    for copy in kept:
        copy.wait()
    sent = outgoing.at[pl.ds(0, parts - 1)]
    pltpu.make_async_copy(sent, sent, part_send).wait()


def forward(send_rows, nodes, w_in, w_out, vectors, parts, chans):
    quarter, node_rows = nodes.shape
    slots = send_rows.shape[0]
    rows = parts * slots // 2
    copies = 3 * (4 + GROUPS)
    like = lambda array: jax.ShapeDtypeStruct((chans * array.shape[0], array.shape[1]), array.dtype)
    return pl.pallas_call(
        functools.partial(forward_kernel, parts=parts, chans=chans),
        in_specs=[pl.BlockSpec(memory_space=pltpu.SMEM)] + [VMEM] * 4,
        out_specs=[ANY] * 5,
        out_shape=[
            like(nodes), jax.ShapeDtypeStruct((chans, rows, LANES), HALF), like(w_in), like(w_out), like(vectors)
        ],
        scratch_shapes=[
            pltpu.VMEM((node_rows, LANES), FLOAT),
            pltpu.VMEM((rows, LANES), FLOAT),
            pltpu.VMEM((parts, slots // 2, LANES), HALF),
            pltpu.SemaphoreType.DMA,
            pltpu.SemaphoreType.DMA((GROUPS,)),
            pltpu.SemaphoreType.DMA((copies,)),
            pltpu.SemaphoreType.DMA((copies,)),
            pltpu.SemaphoreType.DMA((4,)),
        ],
        compiler_params=pltpu.CompilerParams(
            collective_id=0, has_side_effects=True, vmem_limit_bytes=24 * 2**20
        ),
        name="forward",
    )(send_rows, nodes, w_in, w_out, vectors)


def edge_kernel(
    senders, receivers, live, own, halo, edges, w_in, b_in, w_out, b_out, gain, shift,
    edge_new, sums, sent, received, gathered, messages, *partial,
):
    step = pl.program_id(0)
    tile, latent = edges.shape
    node_rows = own.shape[1]
    chans, halo_rows, _ = halo.shape
    quarter = latent // chans
    slots = 16

    @pl.when(step == 0)
    def _():
        across = (((0,), (0,)), ((), ()))
        for start in range(0, node_rows, CHUNK):
            block = own[:, start : start + CHUNK]
            for target, first in ((sent, latent), (received, 2 * latent)):
                result = lax.dot_general(
                    block, w_in[first : first + latent, :], across, preferred_element_type=FLOAT
                )
                target[pl.ds(2 * start, CHUNK, stride=2), :] = result[:, :LANES]
                target[pl.ds(2 * start + 1, CHUNK, stride=2), :] = result[:, LANES:]
        weights = [w_in[2 * latent + c * quarter : 2 * latent + (c + 1) * quarter, :] for c in range(chans)]
        zero = jnp.zeros_like(weights[0])
        halves = []
        for side in range(2):
            padded = [[w, zero] if side == 0 else [zero, w] for w in weights]
            halves.append([
                jnp.concatenate(padded[c] + padded[c + 1], axis=0) for c in range(0, chans, 2)
            ])
        for start in range(0, halo_rows, CHUNK):
            blocks = [
                jnp.concatenate([halo[c, start : start + CHUNK, :], halo[c + 1, start : start + CHUNK, :]], axis=1)
                for c in range(0, chans, 2)
            ]
            for side in range(2):
                result = sum(
                    jnp.dot(b, w, preferred_element_type=FLOAT) for b, w in zip(blocks, halves[side])
                )
                for lanes in range(2):
                    part = result[:, lanes * LANES : (lanes + 1) * LANES].reshape(CHUNK // slots, 2, 8, LANES)
                    for g in range(2):
                        at = node_rows + (2 * side + g) * (halo_rows // 2) + start // 2
                        received[pl.ds(2 * at + lanes, CHUNK // 2, stride=2), :] = part[:, g].reshape(
                            CHUNK // 2, LANES
                        )
        for part in partial:
            part[...] = jnp.zeros_like(part)

    base = step * tile

    def gather(k, carry):
        for u in range(UNROLL):
            j = k * UNROLL + u
            s = senders[base + j]
            r = receivers[base + j]
            gathered[pl.ds(2 * j, 2), :] = sent[pl.ds(2 * s, 2), :] + received[pl.ds(2 * r, 2), :]
        return carry

    lax.fori_loop(0, tile // UNROLL, gather, 0)

    latents = edges[...]
    pre = jnp.dot(latents, w_in[:latent, :], preferred_element_type=FLOAT)
    low = pre[:, :LANES] + gathered[pl.ds(0, tile, stride=2), :]
    high = pre[:, LANES:] + gathered[pl.ds(1, tile, stride=2), :]
    hidden = silu_rows(jnp.concatenate([low, high], axis=1) + b_in[...]).astype(HALF)
    post = jnp.dot(hidden, w_out[...], preferred_element_type=FLOAT) + b_out[...]
    centred = post - jnp.mean(post, axis=-1, keepdims=True)
    var = jnp.mean(centred * centred, axis=-1, keepdims=True)
    norm = centred * lax.rsqrt(var + 1e-05) * gain[...] + shift[...]
    row = lax.broadcasted_iota(jnp.int32, (tile, 1), 0) + base
    norm = jnp.where(row < live[0], norm, 0.0)
    new = (latents.astype(FLOAT) + norm).astype(HALF)
    edge_new[...] = new
    full = new.astype(FLOAT)
    messages[pl.ds(0, tile, stride=2), :] = full[:, :LANES]
    messages[pl.ds(1, tile, stride=2), :] = full[:, LANES:]

    def add_row(j, part):
        rows = pl.ds(2 * receivers[base + j], 2)
        part[rows, :] = part[rows, :] + messages[pl.ds(2 * j, 2), :]

    def scatter(k, carry):
        for u in range(UNROLL):
            add_row(k * UNROLL + u, partial[u % COPIES])
        return carry

    def scatter_one(j, carry):
        add_row(j, partial[0])
        return carry

    count = jnp.clip(live[0] - base, 0, tile)
    whole = count // UNROLL
    lax.fori_loop(0, whole, scatter, 0)
    lax.fori_loop(whole * UNROLL, count, scatter_one, 0)

    @pl.when(step == pl.num_programs(0) - 1)
    def _():
        def chunk(k, carry):
            rows = pl.ds(pl.multiple_of(k * CHUNK, CHUNK), CHUNK)
            total = partial[0][rows, :]
            for part in partial[1:]:
                total += part[rows, :]
            sums[rows, :] = total.astype(sums.dtype)
            return carry

        lax.fori_loop(0, sums.shape[0] // CHUNK, chunk, 0)


def edge_block(senders, receivers, live, own, halo, edges, w_in, b_in, w_out, b_out, gain, shift):
    edge_rows, latent = edges.shape
    node_rows = own.shape[1]
    table_rows = node_rows + 2 * halo.shape[1]
    tile = EDGE_TILE
    full = lambda array: pl.BlockSpec(array.shape, lambda i, *_: (0,) * array.ndim)
    tiled = pl.BlockSpec((tile, latent), lambda i, *_: (i, 0))
    scratch = lambda rows: pltpu.VMEM((2 * rows, LANES), FLOAT)
    b_in, b_out, gain, shift = (v.reshape(1, latent) for v in (b_in, b_out, gain, shift))
    return pl.pallas_call(
        edge_kernel,
        grid_spec=pltpu.PrefetchScalarGridSpec(
            num_scalar_prefetch=3,
            grid=(edge_rows // tile,),
            in_specs=[full(own), full(halo), tiled, full(w_in), full(b_in), full(w_out)] + [full(b_in)] * 3,
            out_specs=[tiled, pl.BlockSpec((2 * table_rows, LANES), lambda i, *_: (0, 0))],
            scratch_shapes=[scratch(node_rows), scratch(table_rows), scratch(tile), scratch(tile)]
            + [scratch(table_rows)] * COPIES,
        ),
        out_shape=[
            jax.ShapeDtypeStruct((edge_rows, latent), HALF),
            jax.ShapeDtypeStruct((2 * table_rows, LANES), HALF),
        ],
        compiler_params=pltpu.CompilerParams(vmem_limit_bytes=54 * 2**20),
        name="edges",
    )(senders, receivers, live, own, halo, edges, w_in, b_in, w_out, b_out, gain, shift)


def reverse_kernel(
    sums, own, rows_of, w_in, w_out, vectors,
    result,
    halo_in, own_in, halo_out, own_out, halo_far, own_far, reduced, returned, spread, own_sum, pick, nodes, fresh,
    part_send, part_recv, send, recv, local,
    *, parts, chans,
):
    dom = lax.axis_index("dom")
    chan = lax.axis_index("chan")
    side = chan // 2
    core = lax.rem(chan, 2)
    other = 1 - side
    far = lax.rem(chan + 2, chans)
    sibling = (dom, chan + 1 - 2 * core)
    across = (dom, far)
    latent, count = nodes.shape
    own_rows = 2 * count
    halo_rows = reduced.shape[0]
    slots = halo_rows // parts
    halo_first = chans * own_rows

    def own_block(index):
        return pl.ds(pl.multiple_of(index * own_rows, own_rows), own_rows)

    def halo_block(index):
        return pl.ds(pl.multiple_of(halo_first + index * halo_rows, halo_rows), halo_rows)

    def push(src, dst, index, target):
        copy = pltpu.make_async_remote_copy(
            src_ref=src, dst_ref=dst, send_sem=send.at[index], recv_sem=recv.at[index],
            device_id=target, device_id_type=MESH,
        )
        copy.start()
        return copy

    columns = pl.ds(pl.multiple_of(chan * count, count), count)
    load = pltpu.make_async_copy(own.at[:, columns], nodes, local.at[0])
    load.start()
    enter(dom, chan, parts, chans)

    halo_pair = [push(sums.at[halo_block(2 * s + 1 - core), :], halo_in.at[s], s, sibling) for s in range(2)]
    own_pair = [push(sums.at[own_block(2 * s + 1 - core), :], own_in.at[s], 2 + s, sibling) for s in range(2)]
    for copy in halo_pair:
        copy.wait()
    halo_out[...] = (
        sums[halo_block(2 * other + core), :].astype(FLOAT) + halo_in[other].astype(FLOAT)
    ).astype(HALF)
    halo_cross = push(halo_out, halo_far, 4, across)
    for copy in own_pair:
        copy.wait()
    own_out[...] = (
        sums[own_block(2 * other + core), :].astype(FLOAT) + own_in[other].astype(FLOAT)
    ).astype(HALF)
    own_cross = push(own_out, own_far, 5, across)

    halo_cross.wait()
    reduced[...] = (
        sums[halo_block(chan), :].astype(FLOAT) + halo_in[side].astype(FLOAT) + halo_far[...].astype(FLOAT)
    ).astype(HALF)

    def send_part(k, carry):
        rows = pl.ds(pl.multiple_of(k * slots, slots), slots)
        pltpu.make_async_remote_copy(
            src_ref=reduced.at[rows, :], dst_ref=returned.at[chan, rows, :],
            send_sem=part_send, recv_sem=part_recv,
            device_id=(lax.rem(dom + 2 * parts - 1 - k, parts), chan), device_id_type=MESH,
        ).start()
        return carry

    lax.fori_loop(0, parts - 1, send_part, 0)
    last = pl.ds((parts - 1) * slots, slots)
    returned[chan, last, :] = reduced[last, :]

    tall = 128
    for start in range(0, count, tall):
        row = lax.broadcasted_iota(jnp.int32, (tall, 1), 0) + (start + chan * count)
        pick[pl.ds(start, tall), :] = jnp.where(rows_of[...] == row, 1.0, 0.0).astype(HALF)

    own_cross.wait()
    own_sum[...] = (
        sums[own_block(chan), :].astype(FLOAT) + own_in[side].astype(FLOAT) + own_far[...].astype(FLOAT)
    )

    arrived = returned.at[chan, pl.ds(0, (parts - 1) * slots), :]
    pltpu.make_async_copy(arrived, arrived, part_recv).wait()
    ring = [push(returned.at[chan], returned.at[chan], 6, across), push(returned.at[chan], returned.at[chan], 7, sibling)]
    ring[0].wait_recv()
    ring.append(push(returned.at[far], returned.at[far], 8, sibling))
    ring[1].wait()
    ring[2].wait()
    ring[0].wait_send()
    for c in range(chans):
        spread[pl.ds(c * halo_rows, halo_rows), :] = returned[c].astype(FLOAT)
    slot_total = chans * halo_rows // 2
    values = jnp.concatenate(
        [spread[pl.ds(0, slot_total, stride=2), :], spread[pl.ds(1, slot_total, stride=2), :]], axis=1
    ).astype(HALF)
    summed = jnp.concatenate([own_sum[pl.ds(0, count, stride=2), :], own_sum[pl.ds(1, count, stride=2), :]], axis=1)
    summed = summed + jnp.dot(pick[...], values, preferred_element_type=FLOAT)
    summed = summed.astype(HALF)

    load.wait()
    latents = nodes[...]
    pre = jnp.dot(w_in[:, :latent], latents, preferred_element_type=FLOAT)
    pre += lax.dot_general(
        w_in[:, latent:], summed, (((1,), (1,)), ((), ())), preferred_element_type=FLOAT
    )
    hidden = silu_rows(pre + vectors[:, 0:1]).astype(HALF)
    post = lax.dot_general(
        w_out[...], hidden, (((0,), (0,)), ((), ())), preferred_element_type=FLOAT
    ) + vectors[:, 3:4]
    centred = post - jnp.mean(post, axis=0, keepdims=True)
    var = jnp.mean(centred * centred, axis=0, keepdims=True)
    norm = centred * lax.rsqrt(var + 1e-05) * vectors[:, 1:2] + vectors[:, 2:3]
    fresh[...] = (latents.astype(FLOAT) + norm).astype(HALF)

    quarter = latent // chans

    def piece(index):
        return fresh.at[pl.ds(pl.multiple_of(index * quarter, quarter), quarter), :]

    keep = pltpu.make_async_copy(piece(chan), result.at[:, columns], local.at[1])
    keep.start()
    final = []
    for k in range(1, chans):
        to = lax.rem(chan + k, chans)
        final.append(push(piece(to), result.at[:, columns], 8 + k, (dom, to)))
    for copy in final:
        copy.wait()
    keep.wait()
    sent = reduced.at[pl.ds(0, (parts - 1) * slots), :]
    pltpu.make_async_copy(sent, sent, part_send).wait()


def reverse(sums, own, rows_of, w_in, w_out, vectors, parts, chans):
    latent, node_rows = own.shape
    count = node_rows // chans
    own_rows = 2 * count
    halo_rows = (sums.shape[0] - 2 * node_rows) // chans
    half = lambda *shape: pltpu.VMEM(shape, HALF)
    return pl.pallas_call(
        functools.partial(reverse_kernel, parts=parts, chans=chans),
        in_specs=[VMEM, ANY] + [VMEM] * 4,
        out_specs=VMEM,
        out_shape=jax.ShapeDtypeStruct((latent // chans, node_rows), HALF),
        scratch_shapes=[
            half(2, halo_rows, LANES), half(2, own_rows, LANES),
            half(halo_rows, LANES), half(own_rows, LANES),
            half(halo_rows, LANES), half(own_rows, LANES),
            half(halo_rows, LANES), half(chans, halo_rows, LANES),
            pltpu.VMEM((chans * halo_rows, LANES), FLOAT), pltpu.VMEM((own_rows, LANES), FLOAT),
            half(count, chans * halo_rows // 2), half(latent, count), half(latent, count),
            pltpu.SemaphoreType.DMA,
            pltpu.SemaphoreType.DMA,
            pltpu.SemaphoreType.DMA((12,)),
            pltpu.SemaphoreType.DMA((12,)),
            pltpu.SemaphoreType.DMA((2,)),
        ],
        compiler_params=pltpu.CompilerParams(
            collective_id=1, has_side_effects=True, vmem_limit_bytes=40 * 2**20
        ),
        name="reverse",
    )(sums, own, rows_of, w_in, w_out, vectors)


def body(
    node_latent,
    edge_latent,
    senders,
    receivers,
    edge_count,
    send_list,
    w_edge_in,
    edge_in_bias,
    w_edge_out,
    edge_out_bias,
    edge_gain,
    edge_shift,
    w_node_in,
    node_in_bias,
    w_node_out,
    node_out_bias,
    node_gain,
    node_shift,
):
    node_rows, quarter = node_latent.shape
    parts = lax.axis_size("dom")
    chans = lax.axis_size("chan")
    dom = lax.axis_index("dom")
    chan = lax.axis_index("chan")
    slots = send_list.shape[2]
    group = slots // chans
    edge_rows = edge_latent.shape[0]

    vectors = jnp.stack(
        [
            node_in_bias.astype(FLOAT), node_gain, node_shift,
            lax.dynamic_slice_in_dim(node_out_bias, chan * quarter, quarter, 0),
        ],
        axis=1,
    )
    vectors = jnp.pad(vectors, ((0, 0), (0, LANES - 4)))
    own, halo, all_in, all_out, all_vectors = forward(
        send_list[0].T, node_latent.T, w_node_in.T, w_node_out, vectors, parts, chans
    )

    slot = receivers - node_rows
    place = lax.rem(dom + 2 * parts - 1 - slot // slots, parts)
    slot = slot % slots
    halo_row = node_rows + (slot // group) * (parts * group) + place * group + slot % group
    rows = jnp.where(receivers < node_rows, receivers, halo_row)
    live = jnp.clip(edge_count - chan * edge_rows, 0, edge_rows)
    edge_new, sums = edge_block(
        senders, rows, live, own, halo, edge_latent, w_edge_in, edge_in_bias, w_edge_out,
        edge_out_bias, edge_gain, edge_shift,
    )

    order = lax.rem(dom + 1 + jnp.arange(parts, dtype=jnp.int32), parts)
    rows_of = send_list[0][order].reshape(parts, chans, group).transpose(1, 0, 2).reshape(1, parts * slots)
    node_new = reverse(sums, own, rows_of, all_in, all_out, all_vectors, parts, chans)
    return (node_new.T, edge_new)


def solution(mesh):
    placed = (
        P("dom", "chan"),
        P(("dom", "chan"), None),
        P(("dom", "chan")),
        P(("dom", "chan")),
        P("dom"),
        P("dom", None, None),
        P(),
        P(),
        P(),
        P(),
        P(),
        P(),
        P(None, "chan"),
        P("chan"),
        P("chan", None),
        P(),
        P("chan"),
        P("chan"),
    )
    return jax.shard_map(
        body,
        mesh=mesh,
        in_specs=placed,
        out_specs=(P("dom", "chan"), P(("dom", "chan"), None)),
        check_vma=False,
    )
```

time: 229 us -> 131 us (0.57)
  waiting for transfers between devices: 78.3 us -> 0 us
  Pallas kernels: 38.6 us -> 116 us
  blocking collectives: 52.7 us -> 0 us
  between operations: 14.6 us -> 1.4 us
  starting transfers between devices: 12.5 us -> 0 us
  local copies, waits for them, and re-layouts: 20.9 us -> 9.56 us
  other arithmetic: 7.99 us -> 2.76 us
  matrix products: 2.94 us -> 0 us
    pallas_call x0 -> x2, Pallas kernels: none -> 79.6 us  [the longest x1 43.1 us: reverse(): pl.pallas_call(functools.partial(reverse_kernel, parts=parts, chans=chans...]
    all_to_all x2 -> x0, blocking collectives: 35.8 us -> none  [the longest x1 27 us: body(): lax.all_to_all(outgoing, 'dom', split_axis=0, concat_axis=0, tiled=True)]
    all_gather x1 -> x0, waiting for transfers between devices: 29.7 us -> none  [body(): table = lax.all_gather(table, 'chan', axis=1, tiled=True)]
    unnamed x4 -> x0, waiting for transfers between devices: 22.9 us -> none
    all_gather x2 -> x0, blocking collectives: 16.9 us -> none  [the longest x1 9.09 us: body(): lax.all_gather(jnp.concatenate([w_node_in.T, w_node_out], axis=1), 'chan'...]
    reduce_scatter x1 -> x0, waiting for transfers between devices: 14.7 us -> none  [body(): lax.psum_scatter(local, 'chan', scatter_dimension=0, tiled=True)]
    all_to_all x1 -> x0, starting transfers between devices: 12.4 us -> none  [body(): lax.all_to_all(halo, 'dom', split_axis=0, concat_axis=0, tiled=True)]
    all_to_all x1 -> x0, waiting for transfers between devices: 11 us -> none  [body(): lax.all_to_all(halo, 'dom', split_axis=0, concat_axis=0, tiled=True)]
  transfers between devices with their start and end apart: 4 -> 0, of which waited for: 4 -> 0; matrix products, arithmetic and copies ran while one was open for 2% -> 0% of each run, Pallas kernels for 0% -> 0%
where the time goes in v2:
time: 131 us; the launch traced here: 130 us
  Pallas kernels  116 us (89%)
  local copies, waits for them, and re-layouts  9.56 us (7%)
  other arithmetic  2.76 us (2%)
  between operations  1.4 us (1%)
    pallas_call x1, Pallas kernels, reverse(): pl.pallas_call(functools.partial(reverse_kernel, parts=parts, chans=chans...  43.1 us
    pallas_call x1, Pallas kernels, edge_block(): pl.pallas_call(edge_kernel, grid_spec=pltpu.PrefetchScalarGridSpec(num_sc...  36.8 us
    pallas_call x1, Pallas kernels, forward(): pl.pallas_call(functools.partial(forward_kernel, parts=parts, chans=chans...  36.5 us
    unnamed x21, local copies, waits for them, and re-layouts  8.42 us

profile of v2, /device:TPU:1, one launch (start us, length us, event | category | flops | bytes accessed | tf_op | source)
XLA Modules:
  0.0 130.0 jit_solution(12315513325619086189)
XLA Ops:
  0.6 0.0 copy-start
  0.6 0.7 copy-done
  1.3 0.1 dynamic-slice_bitcast_fusion
  1.4 0.7 bitcast_convert_fusion
  2.0 0.7 pad_maximum_fusion
  2.7 0.1 copy.33
  2.8 0.0 copy-start.5
  2.8 1.0 copy-done.5
  3.8 0.0 copy-start.6
  3.8 0.8 copy-done.6
  4.6 0.0 copy-start.7
  4.7 0.7 copy-done.7
  5.4 0.0 copy-start.9
  5.4 0.8 copy-done.9
  6.1 36.5 %forward.1 = (bf16[256,2560]{1,0:T(8,128)(2,1)S(1)}, bf16[4,1024,128]{2,1,0:T(8,128)(2,1)S(1)}, bf16[256,512]{1,0:T(8,128)(2,1)S(1)}, bf16[256,256]{1,0:T(8,128)(2,1)S(1)}, f32[256,128]{1,0:T(8,128)S(1)}) custom-call(s32[32,64]{1,0:T(8,128)S(1)} %bitcast.26, bf16[64,2560]{1,0:T(8,128)(2,1)S(1)} %bitcast.24, bf16[64,512]{1,0:T(8,128)(2,1)S(1)} %bitcast.25, ...), custom_call_target="tpu_custom_call" | custom-call | tf_op jit(solution)/shard_map/forward/pallas_call | solution.py:145
  42.6 0.0 copy-start.1
  42.6 1.1 copy-done.1
  43.7 0.0 copy-start.4
  43.7 1.0 copy-done.4
  44.7 1.4 %compare_select_fusion.receivers = s32[5376]{0:T(1024)} fusion(s32[5376]{0:T(1024)} %param.21, s32[]{:T(128)S(6)} %sub.30), kind=kLoop, calls=%fused_computation.1 | loop fusion | flops 284928 | bytes 43012 | tf_op jit(solution)/shard_map/jit(_where)/select_n | solution.py:516
  46.7 0.0 copy-start.8
  46.7 0.0 copy-start.2
  46.8 36.8 %edges.2 = (bf16[5376,256]{1,0:T(8,128)(2,1)}, bf16[9216,128]{1,0:T(8,128)(2,1)}) custom-call(s32[5376]{0:T(1024)} %senders.1, s32[5376]{0:T(1024)} %compare_select_fusion.receivers, s32[1]{0:T(128)S(6)} %min.6.live, bf16[256,2560]{1,0:T(8,128)(2,1)} %copy-done.1, bf16[4,1024,128]{2,1,0:T(8,128)(2,1)} %copy-done.4, bf16[5376,256]{1,0:T(8,128)(2,1)} %edges.3, ...), custom_call_target="tpu_custom_call" | custom-call | tf_op jit(solution)/shard_map/edges/pallas_call | solution.py:287
  83.5 0.0 copy-done.8
  83.5 0.1 copy.34
  83.6 0.6 gather_fusion
  84.2 0.1 copy.35
  84.3 0.1 copy.36
  84.4 0.1 reshape.61.rows_of
  84.5 0.0 copy-done.2
  84.5 0.0 copy-start.3
  84.5 1.7 %copy-done.3 = bf16[9216,128]{1,0:T(8,128)(2,1)S(1)} copy-done((bf16[9216,128]{1,0:T(8,128)(2,1)S(1)}, bf16[9216,128]{1,0:T(8,128)(2,1)}, u32[]{:S(2)}) %copy-start.3) | copy-done | bytes 2359320
  86.2 43.1 %reverse.1 = bf16[64,2560]{1,0:T(8,128)(2,1)S(1)} custom-call(bf16[9216,128]{1,0:T(8,128)(2,1)S(1)} %copy-done.3, bf16[256,2560]{1,0:T(8,128)(2,1)S(1)} %copy-done.2, s32[1,2048]{1,0:T(1,128)S(1)} %reshape.61.rows_of, bf16[256,512]{1,0:T(8,128)(2,1)S(1)} %get-tuple-element.12.w_in, bf16[256,256]{1,0:T(8,128)(2,1)S(1)} %get-tuple-element.13.w_out, ...), custom_call_target="tpu_custom_call" | custom-call | tf_op jit(solution)/shard_map/reverse/pallas_call | solution.py:446
  129.3 0.7 copy.39
  (3 shorter events, 0.0 us)
Async XLA Ops:
  0.6 0.7 copy-start
  2.8 1.0 copy-start.5
  3.8 0.8 copy-start.6
  4.6 0.7 copy-start.7
  5.4 0.8 copy-start.9
  42.6 1.1 copy-start.1
  43.7 1.0 copy-start.4
  46.7 36.8 %copy-start.8 = (s32[1,64,32]{1,2,0:T(8,128)S(1)}, s32[1,64,32]{1,2,0:T(8,128)}, u32[]{:S(2)}) copy-start(s32[1,64,32]{1,2,0:T(8,128)} %param.23) | copy-start | bytes 24580
  46.7 37.8 %copy-start.2 = (bf16[256,2560]{1,0:T(8,128)(2,1)S(1)}, bf16[256,2560]{1,0:T(8,128)(2,1)}, u32[]{:S(2)}) copy-start(bf16[256,2560]{1,0:T(8,128)(2,1)} %copy-done.1) | copy-start | bytes 3932164
  84.5 1.7 %copy-start.3 = (bf16[9216,128]{1,0:T(8,128)(2,1)S(1)}, bf16[9216,128]{1,0:T(8,128)(2,1)}, u32[]{:S(2)}) copy-start(bf16[9216,128]{1,0:T(8,128)(2,1)} %get-tuple-element.11.sums) | copy-start | bytes 7077892

commit v3 on v2

v3 whole, which is shorter than its diff:
```python
import functools

import jax
import jax.numpy as jnp
from jax import lax
from jax.experimental import pallas as pl
from jax.experimental.pallas import tpu as pltpu
from jax.sharding import PartitionSpec as P

LANES = 128
EDGE_TILE = 1344
UNROLL = 32
COPIES = 4
CHUNK = 512
GROUPS = 4
STEPS = 5
VMEM_LIMIT = 58 * 2**20
MESH = pl.DeviceIdType.MESH
FLOAT = jnp.float32
HALF = jnp.bfloat16
ANY = pl.BlockSpec(memory_space=pl.ANY)
VMEM = pl.BlockSpec(memory_space=pltpu.VMEM)


def silu_rows(values):
    return values * jax.nn.sigmoid(values)


def offset_of(place, parts):
    return 2 * lax.rem(place, parts // 2) + 1 + place // (parts // 2)


def enter(dom, chan, parts, chans):
    barrier = pltpu.get_barrier_semaphore()

    def greet(k, carry):
        offset = offset_of(k, parts)
        pl.semaphore_signal(
            barrier, inc=1,
            device_id=(lax.rem(dom + offset, parts), lax.rem(chan + 2 * (offset % 2), chans)),
            device_id_type=MESH,
        )
        return carry

    lax.fori_loop(0, parts - 1, greet, 0)
    for k in range(1, chans):
        pl.semaphore_signal(barrier, inc=1, device_id=(dom, lax.rem(chan + k, chans)), device_id_type=MESH)
    pl.semaphore_wait(barrier, parts + chans - 2)


def forward_kernel(
    send_rows, nodes, senders, receivers,
    own, halo, sender_rows, receiver_rows,
    wide, stage, outgoing, part_send, part_recv, send, recv, local,
    *, parts, chans,
):
    dom = lax.axis_index("dom")
    chan = lax.axis_index("chan")
    quarter, node_rows = nodes.shape
    slots = send_rows.shape[0] // 2
    half = parts // 2
    sibling = (dom, chan + 1 - 2 * lax.rem(chan, 2))
    far = lax.rem(chan + 2, chans)
    across = (dom, far)
    enter(dom, chan, parts, chans)

    def block(index):
        return own.at[pl.ds(pl.multiple_of(index * quarter, quarter), quarter), :]

    def push(src, dst, index, target):
        copy = pltpu.make_async_remote_copy(
            src_ref=src, dst_ref=dst, send_sem=send.at[index], recv_sem=recv.at[index],
            device_id=target, device_id_type=MESH,
        )
        copy.start()
        return copy

    crossed = push(nodes, block(chan), 0, across)
    done = [push(nodes, block(chan), 1, sibling)]
    keep = pltpu.make_async_copy(nodes, block(chan), local)
    keep.start()

    for start in range(0, node_rows, LANES):
        piece = nodes[:, start : start + LANES].astype(FLOAT)
        wide[pl.ds(start, LANES), :] = jnp.concatenate([piece, piece], axis=0).T

    left = lax.broadcasted_iota(jnp.int32, (1, LANES), 1) < quarter

    def fill(k):
        peer = lax.rem(dom + offset_of(k, parts), parts)
        base = pl.multiple_of(k * slots, slots)
        rows = []
        for j in range(slots):
            low = wide[pl.ds(send_rows[j, peer], 1), :]
            high = wide[pl.ds(send_rows[j + slots, peer], 1), :]
            rows.append(jnp.where(left, low, high))
        for j in range(slots):
            stage[pl.ds(base + j, 1), :] = rows[j]
        outgoing[k] = stage[pl.ds(base, slots), :].astype(HALF)
        return peer, base

    group = parts // GROUPS

    def send_part(k, carry):
        peer, base = fill(k)
        target = lax.rem(chan + 2 * (1 - k // half), chans)
        pltpu.make_async_remote_copy(
            src_ref=outgoing.at[k], dst_ref=halo.at[chan, pl.ds(base, slots), :],
            send_sem=part_send, recv_sem=part_recv.at[k // group],
            device_id=(peer, target), device_id_type=MESH,
        ).start()
        return carry

    lax.fori_loop(0, parts - 1, send_part, 0)
    _, base = fill(parts - 1)
    mine = pltpu.make_async_copy(
        outgoing.at[parts - 1], halo.at[chan, pl.ds(base, slots), :], part_recv.at[GROUPS - 1]
    )
    mine.start()

    sender_rows[...] = 2 * senders[...]
    index = receivers[...]
    slot = index - node_rows
    offset = (dom + 2 * parts - 1 - (slot >> 5)) & (parts - 1)
    place = (offset >> 1) + half * (offset & 1)
    halo_row = node_rows + ((slot >> 4) & 1) * (parts * slots) + place * slots + (slot & 15)
    receiver_rows[...] = 2 * jnp.where(index < node_rows, index, halo_row)

    crossed.wait_recv()
    done.append(push(block(far), block(far), 2, sibling))
    crossings = []
    for g in range(GROUPS):
        rows = pl.ds(g * group * slots, group * slots)
        here = far if g * group < half else chan
        piece = halo.at[here, rows, :]
        pltpu.make_async_copy(piece, piece, part_recv.at[g]).wait()
        crossings.append(push(piece, piece, 3 + 3 * g, across))
        done.append(push(piece, piece, 4 + 3 * g, sibling))
    for g in range(GROUPS):
        rows = pl.ds(g * group * slots, group * slots)
        there = chan if g * group < half else far
        piece = halo.at[there, rows, :]
        pltpu.make_async_remote_copy(
            src_ref=piece, dst_ref=piece, send_sem=send.at[3 + 3 * g], recv_sem=recv.at[3 + 3 * g],
            device_id=across, device_id_type=MESH,
        ).wait_recv()
        done.append(push(piece, piece, 5 + 3 * g, sibling))
    for copy in done:
        copy.wait()
    crossed.wait_send()
    for copy in crossings:
        copy.wait_send()
    keep.wait()
    sent = outgoing.at[pl.ds(0, parts - 1)]
    pltpu.make_async_copy(sent, sent, part_send).wait()


def forward(send_rows, nodes, senders, receivers, parts, chans):
    quarter, node_rows = nodes.shape
    slots = send_rows.shape[0]
    rows = parts * slots // 2
    copies = 3 * (1 + GROUPS)
    return pl.pallas_call(
        functools.partial(forward_kernel, parts=parts, chans=chans),
        in_specs=[pl.BlockSpec(memory_space=pltpu.SMEM)] + [VMEM] * 3,
        out_specs=[ANY] * 2 + [VMEM] * 2,
        out_shape=[
            jax.ShapeDtypeStruct((chans * quarter, node_rows), HALF),
            jax.ShapeDtypeStruct((chans, rows, LANES), HALF),
            jax.ShapeDtypeStruct(senders.shape, senders.dtype),
            jax.ShapeDtypeStruct(receivers.shape, receivers.dtype),
        ],
        scratch_shapes=[
            pltpu.VMEM((node_rows, LANES), FLOAT),
            pltpu.VMEM((rows, LANES), FLOAT),
            pltpu.VMEM((parts, slots // 2, LANES), HALF),
            pltpu.SemaphoreType.DMA,
            pltpu.SemaphoreType.DMA((GROUPS,)),
            pltpu.SemaphoreType.DMA((copies,)),
            pltpu.SemaphoreType.DMA((copies,)),
            pltpu.SemaphoreType.DMA,
        ],
        compiler_params=pltpu.CompilerParams(
            collective_id=0, has_side_effects=True, vmem_limit_bytes=VMEM_LIMIT
        ),
        name="forward",
    )(send_rows, nodes, senders, receivers)


def edge_kernel(
    senders, receivers, live, own, halo, edges, w_in, b_in, w_out, b_out, gain, shift,
    edge_new, sums, sent, received, gathered, messages, *partial,
):
    step = pl.program_id(0)
    tile, latent = edges.shape
    node_rows = own.shape[1]
    chans, halo_rows, _ = halo.shape
    quarter = latent // chans

    @pl.when(step == 0)
    def _():
        across = (((0,), (0,)), ((), ()))
        for start in range(0, node_rows, CHUNK):
            block = own[:, start : start + CHUNK]
            for target, first in ((sent, latent), (received, 2 * latent)):
                result = lax.dot_general(
                    block, w_in[first : first + latent, :], across, preferred_element_type=FLOAT
                )
                target[pl.ds(2 * start, CHUNK, stride=2), :] = result[:, :LANES]
                target[pl.ds(2 * start + 1, CHUNK, stride=2), :] = result[:, LANES:]
        weights = [w_in[2 * latent + c * quarter : 2 * latent + (c + 1) * quarter, :] for c in range(chans)]
        zero = jnp.zeros_like(weights[0])
        halves = []
        for side in range(2):
            padded = [[w, zero] if side == 0 else [zero, w] for w in weights]
            halves.append([
                jnp.concatenate(padded[c] + padded[c + 1], axis=0) for c in range(0, chans, 2)
            ])
        for start in range(0, halo_rows, CHUNK):
            blocks = [
                jnp.concatenate([halo[c, start : start + CHUNK, :], halo[c + 1, start : start + CHUNK, :]], axis=1)
                for c in range(0, chans, 2)
            ]
            for side in range(2):
                result = sum(
                    jnp.dot(b, w, preferred_element_type=FLOAT) for b, w in zip(blocks, halves[side])
                )
                at = 2 * (node_rows + side * halo_rows + start)
                received[pl.ds(at, CHUNK, stride=2), :] = result[:, :LANES]
                received[pl.ds(at + 1, CHUNK, stride=2), :] = result[:, LANES:]
        for part in partial:
            part[...] = jnp.zeros_like(part)

    base = step * tile

    def gather(k, carry):
        first = k * UNROLL
        rows = []
        for u in range(UNROLL):
            s = senders[base + first + u]
            r = receivers[base + first + u]
            rows.append(sent[pl.ds(s, 2), :] + received[pl.ds(r, 2), :])
        for u in range(UNROLL):
            gathered[pl.ds(2 * (first + u), 2), :] = rows[u]
        return carry

    lax.fori_loop(0, tile // UNROLL, gather, 0)

    latents = edges[...]
    pre = jnp.dot(latents, w_in[:latent, :], preferred_element_type=FLOAT)
    low = pre[:, :LANES] + gathered[pl.ds(0, tile, stride=2), :]
    high = pre[:, LANES:] + gathered[pl.ds(1, tile, stride=2), :]
    hidden = silu_rows(jnp.concatenate([low, high], axis=1) + b_in[...]).astype(HALF)
    post = jnp.dot(hidden, w_out[...], preferred_element_type=FLOAT) + b_out[...]
    centred = post - jnp.mean(post, axis=-1, keepdims=True)
    var = jnp.mean(centred * centred, axis=-1, keepdims=True)
    norm = centred * lax.rsqrt(var + 1e-05) * gain[...] + shift[...]
    row = lax.broadcasted_iota(jnp.int32, (tile, 1), 0) + base
    norm = jnp.where(row < live[0], norm, 0.0)
    new = (latents.astype(FLOAT) + norm).astype(HALF)
    edge_new[...] = new
    full = new.astype(FLOAT)
    messages[pl.ds(0, tile, stride=2), :] = full[:, :LANES]
    messages[pl.ds(1, tile, stride=2), :] = full[:, LANES:]

    def scatter(k, carry):
        first = k * UNROLL
        rows = [messages[pl.ds(2 * (first + u), 2), :] for u in range(UNROLL)]
        places = [pl.ds(receivers[base + first + u], 2) for u in range(UNROLL)]
        for start in range(0, UNROLL, COPIES):
            new_rows = [partial[u][places[start + u], :] + rows[start + u] for u in range(COPIES)]
            for u in range(COPIES):
                partial[u][places[start + u], :] = new_rows[u]
        return carry

    def scatter_one(j, carry):
        rows = pl.ds(receivers[base + j], 2)
        partial[0][rows, :] = partial[0][rows, :] + messages[pl.ds(2 * j, 2), :]
        return carry

    count = jnp.clip(live[0] - base, 0, tile)
    whole = count // UNROLL
    lax.fori_loop(0, whole, scatter, 0)
    lax.fori_loop(whole * UNROLL, count, scatter_one, 0)

    @pl.when(step == pl.num_programs(0) - 1)
    def _():
        table_rows = sums.shape[0] // 2

        def chunk(k, carry):
            start = pl.multiple_of(k * CHUNK, CHUNK)
            for lanes in range(2):
                rows = pl.ds(2 * start + lanes, CHUNK, stride=2)
                total = partial[0][rows, :]
                for part in partial[1:]:
                    total += part[rows, :]
                sums[pl.ds(lanes * table_rows + start, CHUNK), :] = total.astype(sums.dtype)
            return carry

        lax.fori_loop(0, table_rows // CHUNK, chunk, 0)


def edge_block(senders, receivers, live, own, halo, edges, w_in, b_in, w_out, b_out, gain, shift):
    edge_rows, latent = edges.shape
    node_rows = own.shape[1]
    table_rows = node_rows + 2 * halo.shape[1]
    tile = EDGE_TILE
    full = lambda array: pl.BlockSpec(array.shape, lambda i, *_: (0,) * array.ndim)
    tiled = pl.BlockSpec((tile, latent), lambda i, *_: (i, 0))
    scratch = lambda rows: pltpu.VMEM((2 * rows, LANES), FLOAT)
    b_in, b_out, gain, shift = (v.reshape(1, latent) for v in (b_in, b_out, gain, shift))
    return pl.pallas_call(
        edge_kernel,
        grid_spec=pltpu.PrefetchScalarGridSpec(
            num_scalar_prefetch=3,
            grid=(edge_rows // tile,),
            in_specs=[full(own), full(halo), tiled, full(w_in), full(b_in), full(w_out)] + [full(b_in)] * 3,
            out_specs=[tiled, pl.BlockSpec((2 * table_rows, LANES), lambda i, *_: (0, 0))],
            scratch_shapes=[scratch(node_rows), scratch(table_rows), scratch(tile), scratch(tile)]
            + [scratch(table_rows)] * COPIES,
        ),
        out_shape=[
            jax.ShapeDtypeStruct((edge_rows, latent), HALF),
            jax.ShapeDtypeStruct((2 * table_rows, LANES), HALF),
        ],
        compiler_params=pltpu.CompilerParams(vmem_limit_bytes=VMEM_LIMIT),
        name="edges",
    )(senders, receivers, live, own, halo, edges, w_in, b_in, w_out, b_out, gain, shift)


def reverse_kernel(
    sums, own, rows_of, w_in, w_out, vectors,
    result,
    halo_in, own_in, halo_mine, own_mine, halo_out, own_out, halo_far, own_far, reduced, returned,
    own_sum, pick, nodes, summed, fresh, all_in, all_out, all_vectors,
    part_send, part_recv, send, recv, local, row_send, row_recv,
    *, parts, chans,
):
    dom = lax.axis_index("dom")
    chan = lax.axis_index("chan")
    side = chan // 2
    core = lax.rem(chan, 2)
    half = lax.rem(side + dom, 2)
    other = 1 - half
    far = lax.rem(chan + 2, chans)
    sibling = (dom, chan + 1 - 2 * core)
    across = (dom, far)
    latent, count = nodes.shape
    quarter = latent // chans
    halo_rows = reduced.shape[0]
    slots = halo_rows // parts
    table_rows = sums.shape[0] // 2

    def own_block(lanes, index):
        return sums.at[pl.ds(pl.multiple_of(lanes * table_rows + index * count, LANES), count), :]

    def halo_block(lanes, index):
        start = pl.multiple_of(lanes * table_rows + 2 * count + index * halo_rows, LANES)
        return sums.at[pl.ds(start, halo_rows), :]

    def push(src, dst, index, target):
        copy = pltpu.make_async_remote_copy(
            src_ref=src, dst_ref=dst, send_sem=send.at[index], recv_sem=recv.at[index],
            device_id=target, device_id_type=MESH,
        )
        copy.start()
        return copy

    def fetch(src, dst, index):
        copy = pltpu.make_async_copy(src, dst, local.at[index])
        copy.start()
        return copy

    columns = pl.ds(pl.multiple_of(core * count, count), count)
    halo_mine_in = [fetch(halo_block(s, core), halo_mine.at[s], s) for s in range(2)]
    own_mine_in = [fetch(own_block(s, core), own_mine.at[s], 2 + s) for s in range(2)]
    load = fetch(own.at[:, columns], nodes, 4)
    enter(dom, chan, parts, chans)

    halo_pair = [push(halo_block(s, 1 - core), halo_in.at[s], s, sibling) for s in range(2)]
    own_pair = [push(own_block(s, 1 - core), own_in.at[s], 2 + s, sibling) for s in range(2)]
    weights = [(w_in, all_in), (w_out, all_out), (vectors, all_vectors)]
    weight_crossed, weight_done = [], []
    for n, (src, dst) in enumerate(weights):
        weight_crossed.append(push(src, dst.at[chan], 6 + 3 * n, across))
        weight_done.append(push(src, dst.at[chan], 7 + 3 * n, sibling))
        dst[chan] = src[...]

    for copy in halo_mine_in + halo_pair:
        copy.wait()
    halo_out[...] = (halo_mine[other].astype(FLOAT) + halo_in[other].astype(FLOAT)).astype(HALF)
    halo_cross = push(halo_out, halo_far, 4, across)
    for copy in own_mine_in + own_pair:
        copy.wait()
    own_out[...] = (own_mine[other].astype(FLOAT) + own_in[other].astype(FLOAT)).astype(HALF)
    own_cross = push(own_out, own_far, 5, across)

    halo_cross.wait()
    reduced[...] = (
        halo_mine[half].astype(FLOAT) + halo_in[half].astype(FLOAT) + halo_far[...].astype(FLOAT)
    ).astype(HALF)

    def send_part(k, carry):
        offset = offset_of(k, parts)
        rows = pl.ds(pl.multiple_of(k * slots, slots), slots)
        pltpu.make_async_remote_copy(
            src_ref=reduced.at[rows, :], dst_ref=returned.at[core, rows, :],
            send_sem=part_send, recv_sem=part_recv.at[k // (parts // GROUPS)],
            device_id=(lax.rem(dom + parts - offset, parts), lax.rem(chan + 2 * (offset % 2), chans)),
            device_id_type=MESH,
        ).start()
        return carry

    lax.fori_loop(0, parts - 1, send_part, 0)
    last = pl.ds((parts - 1) * slots, slots)
    mine = pltpu.make_async_copy(reduced.at[last, :], returned.at[core, last, :], part_recv.at[GROUPS - 1])
    mine.start()

    def choose(n, carry):
        start = pl.multiple_of(n * LANES, LANES)
        row = lax.broadcasted_iota(jnp.int32, (LANES, 1), 0) + (start + core * count)
        pick[pl.ds(start, LANES), :] = jnp.where(rows_of[...] == row, 1.0, 0.0).astype(HALF)
        return carry

    lax.fori_loop(0, count // LANES, choose, 0)

    for n, (src, dst) in enumerate(weights):
        weight_crossed[n].wait()
        weight_done.append(push(dst.at[far], dst.at[far], 8 + 3 * n, sibling))

    own_cross.wait()
    own_sum[...] = own_mine[half].astype(FLOAT) + own_in[half].astype(FLOAT) + own_far[...].astype(FLOAT)

    group_rows = halo_rows // GROUPS
    pairs = []
    for g in range(GROUPS):
        rows = pl.ds(g * group_rows, group_rows)
        piece = returned.at[core, rows, :]
        pltpu.make_async_copy(piece, piece, part_recv.at[g]).wait()
        pairs.append(push(piece, piece, 15 + g, sibling))
    for copy in pairs + weight_done:
        copy.wait()

    values = returned[...].reshape(2 * halo_rows, LANES)
    pieces = range(0, count, count // STEPS)
    sent = []
    for n, start in enumerate(pieces):
        rows = pl.ds(start, count // STEPS)
        total = own_sum[rows, :] + jnp.dot(pick[rows, :], values, preferred_element_type=FLOAT)
        summed[half, rows, :] = total.astype(HALF)
        piece = summed.at[half, rows, :]
        copy = pltpu.make_async_remote_copy(
            src_ref=piece, dst_ref=piece, send_sem=row_send.at[n], recv_sem=row_recv.at[n],
            device_id=across, device_id_type=MESH,
        )
        copy.start()
        sent.append(copy)

    load.wait()
    first_layer = all_in[...].reshape(latent, 2 * latent)
    second_layer = all_out[...].reshape(latent, latent)
    vector = all_vectors[...].reshape(latent, LANES)
    both = (((1,), (1,)), ((), ()))
    for n, start in enumerate(pieces):
        rows = pl.ds(start, count // STEPS)
        latents = nodes[:, rows]
        pre = jnp.dot(first_layer[:, :latent], latents, preferred_element_type=FLOAT)
        piece = summed.at[other, rows, :]
        pltpu.make_async_remote_copy(
            src_ref=piece, dst_ref=piece, send_sem=row_send.at[n], recv_sem=row_recv.at[n],
            device_id=across, device_id_type=MESH,
        ).wait_recv()
        total = jnp.concatenate([summed[0, rows, :], summed[1, rows, :]], axis=1)
        pre += lax.dot_general(first_layer[:, latent:], total, both, preferred_element_type=FLOAT)
        hidden = silu_rows(pre + vector[:, 0:1]).astype(HALF)
        post = lax.dot_general(
            second_layer, hidden, (((0,), (0,)), ((), ())), preferred_element_type=FLOAT
        ) + vector[:, 3:4]
        centred = post - jnp.mean(post, axis=0, keepdims=True)
        var = jnp.mean(centred * centred, axis=0, keepdims=True)
        norm = centred * lax.rsqrt(var + 1e-05) * vector[:, 1:2] + vector[:, 2:3]
        new = (latents.astype(FLOAT) + norm).astype(HALF)
        for c in range(chans):
            fresh[c, :, rows] = new[c * quarter : (c + 1) * quarter, :]

    keep = fetch(fresh.at[chan], result.at[:, columns], 5)
    final = push(fresh.at[chan + 1 - 2 * core], result.at[:, columns], 19, sibling)
    for copy in sent:
        copy.wait_send()
    gone = reduced.at[pl.ds(0, (parts - 1) * slots), :]
    pltpu.make_async_copy(gone, gone, part_send).wait()
    keep.wait()
    final.wait()


def reverse(sums, own, rows_of, w_in, w_out, vectors, parts, chans):
    latent, node_rows = own.shape
    count = node_rows // 2
    halo_rows = (sums.shape[0] - 2 * node_rows) // 4
    half = lambda *shape: pltpu.VMEM(shape, HALF)
    return pl.pallas_call(
        functools.partial(reverse_kernel, parts=parts, chans=chans),
        in_specs=[ANY, ANY] + [VMEM] * 4,
        out_specs=VMEM,
        out_shape=jax.ShapeDtypeStruct((latent // chans, node_rows), HALF),
        scratch_shapes=[
            half(2, halo_rows, LANES), half(2, count, LANES),
            half(2, halo_rows, LANES), half(2, count, LANES),
            half(halo_rows, LANES), half(count, LANES),
            half(halo_rows, LANES), half(count, LANES),
            half(halo_rows, LANES), half(2, halo_rows, LANES),
            pltpu.VMEM((count, LANES), FLOAT),
            half(count, 2 * halo_rows), half(latent, count), half(2, count, LANES),
            half(chans, latent // chans, count),
            half(chans, *w_in.shape), half(chans, *w_out.shape), pltpu.VMEM((chans, *vectors.shape), FLOAT),
            pltpu.SemaphoreType.DMA,
            pltpu.SemaphoreType.DMA((GROUPS,)),
            pltpu.SemaphoreType.DMA((20,)),
            pltpu.SemaphoreType.DMA((20,)),
            pltpu.SemaphoreType.DMA((6,)),
            pltpu.SemaphoreType.DMA((STEPS,)),
            pltpu.SemaphoreType.DMA((STEPS,)),
        ],
        compiler_params=pltpu.CompilerParams(
            collective_id=1, has_side_effects=True, vmem_limit_bytes=VMEM_LIMIT
        ),
        name="reverse",
    )(sums, own, rows_of, w_in, w_out, vectors)


def body(
    node_latent,
    edge_latent,
    senders,
    receivers,
    edge_count,
    send_list,
    w_edge_in,
    edge_in_bias,
    w_edge_out,
    edge_out_bias,
    edge_gain,
    edge_shift,
    w_node_in,
    node_in_bias,
    w_node_out,
    node_out_bias,
    node_gain,
    node_shift,
):
    node_rows, quarter = node_latent.shape
    parts = lax.axis_size("dom")
    chans = lax.axis_size("chan")
    dom = lax.axis_index("dom")
    chan = lax.axis_index("chan")
    slots = send_list.shape[2]
    edge_rows = edge_latent.shape[0]

    vectors = jnp.stack(
        [
            node_in_bias.astype(FLOAT), node_gain, node_shift,
            lax.dynamic_slice_in_dim(node_out_bias, chan * quarter, quarter, 0),
        ],
        axis=1,
    )
    vectors = jnp.pad(vectors, ((0, 0), (0, LANES - 4)))
    own, halo, sender_rows, receiver_rows = forward(
        send_list[0].T, node_latent.T, senders.reshape(-1, LANES), receivers.reshape(-1, LANES), parts, chans
    )
    live = jnp.clip(edge_count - chan * edge_rows, 0, edge_rows)
    edge_new, sums = edge_block(
        sender_rows.reshape(-1), receiver_rows.reshape(-1), live, own, halo, edge_latent, w_edge_in,
        edge_in_bias, w_edge_out, edge_out_bias, edge_gain, edge_shift,
    )

    source = lax.rem(dom + offset_of(jnp.arange(parts, dtype=jnp.int32), parts), parts)
    rows_of = send_list[0][source].reshape(parts, 2, slots // 2).transpose(1, 0, 2).reshape(1, parts * slots)
    node_new = reverse(sums, own, rows_of, w_node_in.T, w_node_out, vectors, parts, chans)
    return (node_new.T, edge_new)


def solution(mesh):
    placed = (
        P("dom", "chan"),
        P(("dom", "chan"), None),
        P(("dom", "chan")),
        P(("dom", "chan")),
        P("dom"),
        P("dom", None, None),
        P(),
        P(),
        P(),
        P(),
        P(),
        P(),
        P(None, "chan"),
        P("chan"),
        P("chan", None),
        P(),
        P("chan"),
        P("chan"),
    )
    return jax.shard_map(
        body,
        mesh=mesh,
        in_specs=placed,
        out_specs=(P("dom", "chan"), P(("dom", "chan"), None)),
        check_vma=False,
    )
```

time: 131 us -> 107 us (0.82)
  Pallas kernels: 116 us -> 101 us
  local copies, waits for them, and re-layouts: 9.56 us -> 4.09 us
  other arithmetic: 2.76 us -> 0.04 us
    pallas_call x1, Pallas kernels: 36.8 us -> 28.7 us  [edge_block(): pl.pallas_call(edge_kernel, grid_spec=pltpu.PrefetchScalarGridSpec(num_sc...]
    unnamed x21 -> x11, local copies, waits for them, and re-layouts: 8.42 us -> 1.75 us
    pallas_call x1, Pallas kernels: 36.5 us -> 32.3 us  [forward(): pl.pallas_call(functools.partial(forward_kernel, parts=parts, chans=chans...]
    pallas_call x1, Pallas kernels: 43.1 us -> 39.9 us  [reverse(): pl.pallas_call(functools.partial(reverse_kernel, parts=parts, chans=chans...]
    select_n x2 -> x1, other arithmetic: 1.42 us -> 0.02 us  [body(): send_list[0][source].reshape(parts, 2, slots // 2).transpose(1, 0, 2)]
    another operation x2, other arithmetic: 1.34 us -> 0.01 us  [body(): jnp.stack([node_in_bias.astype(FLOAT), node_gain, node_shift, lax.dynamic...]
where the time goes in v3:
time: 107 us; the launch traced here: 106 us
  Pallas kernels  101 us (94%)
  local copies, waits for them, and re-layouts  4.09 us (4%)
  between operations  1.37 us (1%)
    pallas_call x1, Pallas kernels, reverse(): pl.pallas_call(functools.partial(reverse_kernel, parts=parts, chans=chans...  39.9 us
    pallas_call x1, Pallas kernels, forward(): pl.pallas_call(functools.partial(forward_kernel, parts=parts, chans=chans...  32.3 us
    pallas_call x1, Pallas kernels, edge_block(): pl.pallas_call(edge_kernel, grid_spec=pltpu.PrefetchScalarGridSpec(num_sc...  28.7 us

profile of v3, /device:TPU:1, one launch (start us, length us, event | category | flops | bytes accessed | tf_op | source)
XLA Modules:
  0.0 106.3 jit_solution(4957087847503837910)
XLA Ops:
  0.6 0.0 copy-start
  0.6 32.3 %forward.1 = (bf16[256,2560]{1,0:T(8,128)(2,1)}, bf16[4,1024,128]{2,1,0:T(8,128)(2,1)}, s32[42,128]{1,0:T(8,128)}, s32[42,128]{1,0:T(8,128)}) custom-call(s32[32,64]{1,0:T(8,128)} %bitcast.30, bf16[64,2560]{1,0:T(8,128)(2,1)} %bitcast.28, s32[42,128]{1,0:T(8,128)} %bitcast.35, s32[42,128]{1,0:T(8,128)} %bitcast.36), custom_call_target="tpu_custom_call" | custom-call | tf_op jit(solution)/shard_map/forward/pallas_call | solution.py:163
  33.6 0.0 copy-start.4
  33.6 0.0 copy-start.2
  33.6 0.0 copy-start.3
  33.6 0.0 copy-start.1
  33.6 28.7 %edges.2 = (bf16[5376,256]{1,0:T(8,128)(2,1)}, bf16[9216,128]{1,0:T(8,128)(2,1)}) custom-call(s32[5376]{0:T(1024)} %bitcast.33, s32[5376]{0:T(1024)} %bitcast.34, s32[1]{0:T(128)S(6)} %min.6.live, bf16[256,2560]{1,0:T(8,128)(2,1)} %get-tuple-element.10.own, bf16[4,1024,128]{2,1,0:T(8,128)(2,1)} %get-tuple-element.11.halo, bf16[5376,256]{1,0:T(8,128)(2,1)} %edges.3, ...), custom_call_target="tpu_custom_call" | custom-call | tf_op jit(solution)/shard_map/edges/pallas_call | solution.py:312
  62.3 0.0 copy-done
  62.3 0.1 dynamic-slice_bitcast_fusion
  62.4 0.0 copy-done.4
  62.4 0.0 copy-done.2
  62.4 0.0 copy-done.3
  62.4 0.1 copy.36
  62.5 0.6 pad.4.vectors
  63.2 0.0 copy-done.1
  63.2 0.1 copy.33
  63.3 0.6 gather_fusion
  63.9 0.1 copy.34
  64.0 0.1 copy.35
  64.0 0.7 reshape.116.rows_of
  64.7 39.9 %reverse.1 = bf16[64,2560]{1,0:T(8,128)(2,1)} custom-call(bf16[9216,128]{1,0:T(8,128)(2,1)} %get-tuple-element.12.sums, bf16[256,2560]{1,0:T(8,128)(2,1)} %get-tuple-element.10.own, s32[1,2048]{1,0:T(1,128)} %reshape.116.rows_of, bf16[64,512]{1,0:T(8,128)(2,1)} %bitcast.29, bf16[64,256]{1,0:T(8,128)(2,1)} %w_out.3, f32[64,128]{1,0:T(8,128)} %pad.4.vectors), custom_call_target="tpu_custom_call" | custom-call | tf_op jit(solution)/shard_map/reverse/pallas_call | solution.py:501
  104.6 1.7 %copy.39 = bf16[2560,64]{0,1:T(8,128)(2,1)} copy(bf16[2560,64]{0,1:T(8,128)(2,1)} %bitcast.27) | data formatting | bytes 655360
  (4 shorter events, 0.0 us)
Async XLA Ops:
  0.6 61.7 %copy-start = (f32[256]{0:T(256)S(1)}, f32[256]{0:T(256)}, u32[]{:S(2)}) copy-start(f32[256]{0:T(256)} %param.33) | copy-start | bytes 3076
  33.6 28.8 %copy-start.4 = (bf16[64]{0:T(256)(128)(2,1)S(1)}, bf16[64]{0:T(256)(128)(2,1)}, u32[]{:S(2)}) copy-start(bf16[64]{0:T(256)(128)(2,1)} %param.31) | copy-start | bytes 388
  33.6 28.8 %copy-start.2 = (f32[64]{0:T(128)S(1)}, f32[64]{0:T(128)}, u32[]{:S(2)}) copy-start(f32[64]{0:T(128)} %param.35) | copy-start | bytes 772
  33.6 28.8 %copy-start.3 = (f32[64]{0:T(128)S(1)}, f32[64]{0:T(128)}, u32[]{:S(2)}) copy-start(f32[64]{0:T(128)} %param.34) | copy-start | bytes 772
  33.6 29.6 %copy-start.1 = (s32[1,64,32]{1,2,0:T(8,128)S(1)}, s32[1,64,32]{1,2,0:T(8,128)}, u32[]{:S(2)}) copy-start(s32[1,64,32]{1,2,0:T(8,128)} %param.23) | copy-start | bytes 24580

commit v4 on v3

v4 whole, which is shorter than its diff:
```python
import functools

import jax
import jax.numpy as jnp
from jax import lax
from jax.experimental import pallas as pl
from jax.experimental.pallas import tpu as pltpu
from jax.sharding import PartitionSpec as P

LANES = 128
EDGE_TILE = 1344
UNROLL = 32
COPIES = 4
CHUNK = 512
GROUPS = 4
STEPS = 5
VMEM_LIMIT = 58 * 2**20
MESH = pl.DeviceIdType.MESH
FLOAT = jnp.float32
HALF = jnp.bfloat16
ANY = pl.BlockSpec(memory_space=pl.ANY)
VMEM = pl.BlockSpec(memory_space=pltpu.VMEM)


def silu_rows(values):
    return values * jax.nn.sigmoid(values)


def offset_of(place, parts):
    return 2 * lax.rem(place, parts // 2) + 1 + place // (parts // 2)


def enter(dom, chan, parts, chans):
    barrier = pltpu.get_barrier_semaphore()

    def greet(k, carry):
        offset = offset_of(k, parts)
        pl.semaphore_signal(
            barrier, inc=1,
            device_id=(lax.rem(dom + offset, parts), lax.rem(chan + 2 * (offset % 2), chans)),
            device_id_type=MESH,
        )
        return carry

    lax.fori_loop(0, parts - 1, greet, 0)
    for k in range(1, chans):
        pl.semaphore_signal(barrier, inc=1, device_id=(dom, lax.rem(chan + k, chans)), device_id_type=MESH)
    pl.semaphore_wait(barrier, parts + chans - 2)


def forward_kernel(
    send_rows, nodes, senders, receivers,
    own, halo, sender_rows, receiver_rows,
    wide, stage, outgoing, part_send, part_recv, send, recv, local,
    *, parts, chans,
):
    dom = lax.axis_index("dom")
    chan = lax.axis_index("chan")
    quarter, node_rows = nodes.shape
    slots = send_rows.shape[0] // 2
    half = parts // 2
    sibling = (dom, chan + 1 - 2 * lax.rem(chan, 2))
    far = lax.rem(chan + 2, chans)
    across = (dom, far)
    enter(dom, chan, parts, chans)

    def block(index, n):
        rows = pl.ds(pl.multiple_of(index * quarter, quarter), quarter)
        return own.at[rows, n * node_rows // STEPS : (n + 1) * node_rows // STEPS]

    def push(src, dst, index, target):
        copy = pltpu.make_async_remote_copy(
            src_ref=src, dst_ref=dst, send_sem=send.at[index], recv_sem=recv.at[index],
            device_id=target, device_id_type=MESH,
        )
        copy.start()
        return copy

    crossed, done = [], []

    def push_own(n):
        piece = nodes.at[:, n * node_rows // STEPS : (n + 1) * node_rows // STEPS]
        crossed.append(push(piece, block(chan, n), 3 * (GROUPS + n), across))
        done.append(push(piece, block(chan, n), 3 * (GROUPS + n) + 1, sibling))

    rows = pl.ds(pl.multiple_of(chan * quarter, quarter), quarter)
    keep = pltpu.make_async_copy(nodes, own.at[rows, :], local)
    keep.start()
    for n in range(STEPS):
        push_own(n)

    for start in range(0, node_rows, LANES):
        piece = nodes[:, start : start + LANES].astype(FLOAT)
        wide[pl.ds(start, LANES), :] = jnp.concatenate([piece, piece], axis=0).T

    left = lax.broadcasted_iota(jnp.int32, (1, LANES), 1) < quarter

    def fill(k):
        peer = lax.rem(dom + offset_of(k, parts), parts)
        base = pl.multiple_of(k * slots, slots)
        rows = []
        for j in range(slots):
            low = wide[pl.ds(send_rows[j, peer], 1), :]
            high = wide[pl.ds(send_rows[j + slots, peer], 1), :]
            rows.append(jnp.where(left, low, high))
        for j in range(slots):
            stage[pl.ds(base + j, 1), :] = rows[j]
        outgoing[k] = stage[pl.ds(base, slots), :].astype(HALF)
        return peer, base

    group = parts // GROUPS

    def send_part(k, carry):
        peer, base = fill(k)
        target = lax.rem(chan + 2 * (1 - k // half), chans)
        pltpu.make_async_remote_copy(
            src_ref=outgoing.at[k], dst_ref=halo.at[chan, pl.ds(base, slots), :],
            send_sem=part_send, recv_sem=part_recv.at[k // group],
            device_id=(peer, target), device_id_type=MESH,
        ).start()
        return carry

    crossings, pieces = [], []

    def share(g):
        rows = pl.ds(g * group * slots, group * slots)
        here, there = (far, chan) if g * group < half else (chan, far)
        piece = halo.at[here, rows, :]
        pltpu.make_async_copy(piece, piece, part_recv.at[g]).wait()
        crossings.append(push(piece, piece, 3 * g, across))
        done.append(push(piece, piece, 1 + 3 * g, sibling))
        pieces.append(halo.at[there, rows, :])

    for g in range(GROUPS):
        lax.fori_loop(g * group, min((g + 1) * group, parts - 1), send_part, 0)
    _, base = fill(parts - 1)
    mine = pltpu.make_async_copy(
        outgoing.at[parts - 1], halo.at[chan, pl.ds(base, slots), :], part_recv.at[GROUPS - 1]
    )
    mine.start()

    sender_rows[...] = 2 * senders[...]
    index = receivers[...]
    slot = index - node_rows
    offset = (dom + 2 * parts - 1 - (slot >> 5)) & (parts - 1)
    place = (offset >> 1) + half * (offset & 1)
    halo_row = node_rows + ((slot >> 4) & 1) * (parts * slots) + place * slots + (slot & 15)
    receiver_rows[...] = 2 * jnp.where(index < node_rows, index, halo_row)

    for g in range(GROUPS):
        share(g)
    for n in range(STEPS):
        crossed[n].wait_recv()
        done.append(push(block(far, n), block(far, n), 3 * (GROUPS + n) + 2, sibling))
    for g, piece in enumerate(pieces):
        pltpu.make_async_remote_copy(
            src_ref=piece, dst_ref=piece, send_sem=send.at[3 * g], recv_sem=recv.at[3 * g],
            device_id=across, device_id_type=MESH,
        ).wait_recv()
        done.append(push(piece, piece, 2 + 3 * g, sibling))
    for copy in done:
        copy.wait()
    for copy in crossed:
        copy.wait_send()
    for copy in crossings:
        copy.wait_send()
    keep.wait()
    sent = outgoing.at[pl.ds(0, parts - 1)]
    pltpu.make_async_copy(sent, sent, part_send).wait()


def forward(send_rows, nodes, senders, receivers, parts, chans):
    quarter, node_rows = nodes.shape
    slots = send_rows.shape[0]
    rows = parts * slots // 2
    copies = 3 * (STEPS + GROUPS)
    return pl.pallas_call(
        functools.partial(forward_kernel, parts=parts, chans=chans),
        in_specs=[pl.BlockSpec(memory_space=pltpu.SMEM)] + [VMEM] * 3,
        out_specs=[ANY] * 2 + [VMEM] * 2,
        out_shape=[
            jax.ShapeDtypeStruct((chans * quarter, node_rows), HALF),
            jax.ShapeDtypeStruct((chans, rows, LANES), HALF),
            jax.ShapeDtypeStruct(senders.shape, senders.dtype),
            jax.ShapeDtypeStruct(receivers.shape, receivers.dtype),
        ],
        scratch_shapes=[
            pltpu.VMEM((node_rows, LANES), FLOAT),
            pltpu.VMEM((rows, LANES), FLOAT),
            pltpu.VMEM((parts, slots // 2, LANES), HALF),
            pltpu.SemaphoreType.DMA,
            pltpu.SemaphoreType.DMA((GROUPS,)),
            pltpu.SemaphoreType.DMA((copies,)),
            pltpu.SemaphoreType.DMA((copies,)),
            pltpu.SemaphoreType.DMA,
        ],
        compiler_params=pltpu.CompilerParams(
            collective_id=0, has_side_effects=True, vmem_limit_bytes=VMEM_LIMIT
        ),
        name="forward",
    )(send_rows, nodes, senders, receivers)


def edge_kernel(
    live, senders_in, receivers_in, own_in, halo_in, edges_in, w_in_in, b_in, w_out, b_out, gain, shift,
    edge_new, sums,
    senders, receivers, own, halo, edges, w_in, fresh, totals, sent, received, gathered, messages, loads, tile_out, sum_out,
    *partial,
):
    tile = messages.shape[0] // 2
    edge_rows, latent = edges.shape
    node_rows = own.shape[1]
    chans, halo_rows, _ = halo.shape
    quarter = latent // chans
    steps = edge_rows // tile

    loading = []
    for n, (src, dst) in enumerate((
        (own_in, own), (w_in_in, w_in), (halo_in, halo), (senders_in, senders), (receivers_in, receivers), (edges_in, edges)
    )):
        loading.append(pltpu.make_async_copy(src, dst, loads.at[n]))
        loading[-1].start()
    for part in partial:
        part[...] = jnp.zeros_like(part)
    loading[0].wait()
    loading[1].wait()
    across = (((0,), (0,)), ((), ()))
    for start in range(0, node_rows, CHUNK):
        block = own[:, start : start + CHUNK]
        for target, first in ((sent, latent), (received, 2 * latent)):
            result = lax.dot_general(
                block, w_in[first : first + latent, :], across, preferred_element_type=FLOAT
            )
            target[pl.ds(2 * start, CHUNK, stride=2), :] = result[:, :LANES]
            target[pl.ds(2 * start + 1, CHUNK, stride=2), :] = result[:, LANES:]
    weights = [w_in[2 * latent + c * quarter : 2 * latent + (c + 1) * quarter, :] for c in range(chans)]
    zero = jnp.zeros_like(weights[0])
    halves = []
    for side in range(2):
        padded = [[w, zero] if side == 0 else [zero, w] for w in weights]
        halves.append([
            jnp.concatenate(padded[c] + padded[c + 1], axis=0) for c in range(0, chans, 2)
        ])
    loading[2].wait()
    for start in range(0, halo_rows, CHUNK):
        blocks = [
            jnp.concatenate([halo[c, start : start + CHUNK, :], halo[c + 1, start : start + CHUNK, :]], axis=1)
            for c in range(0, chans, 2)
        ]
        for side in range(2):
            result = sum(
                jnp.dot(b, w, preferred_element_type=FLOAT) for b, w in zip(blocks, halves[side])
            )
            at = 2 * (node_rows + side * halo_rows + start)
            received[pl.ds(at, CHUNK, stride=2), :] = result[:, :LANES]
            received[pl.ds(at + 1, CHUNK, stride=2), :] = result[:, LANES:]
    for copy in loading[3:]:
        copy.wait()

    def one_tile(step, carry):
        base = pl.multiple_of(step * tile, tile)

        def gather(k, carry):
            first = k * UNROLL
            rows = []
            for u in range(UNROLL):
                s = senders[base + first + u]
                r = receivers[base + first + u]
                rows.append(sent[pl.ds(s, 2), :] + received[pl.ds(r, 2), :])
            for u in range(UNROLL):
                gathered[pl.ds(2 * (first + u), 2), :] = rows[u]
            return carry

        lax.fori_loop(0, tile // UNROLL, gather, 0)

        latents = edges[pl.ds(base, tile), :]
        pre = jnp.dot(latents, w_in[:latent, :], preferred_element_type=FLOAT)
        low = pre[:, :LANES] + gathered[pl.ds(0, tile, stride=2), :]
        high = pre[:, LANES:] + gathered[pl.ds(1, tile, stride=2), :]
        hidden = silu_rows(jnp.concatenate([low, high], axis=1) + b_in[...]).astype(HALF)
        post = jnp.dot(hidden, w_out[...], preferred_element_type=FLOAT) + b_out[...]
        centred = post - jnp.mean(post, axis=-1, keepdims=True)
        var = jnp.mean(centred * centred, axis=-1, keepdims=True)
        norm = centred * lax.rsqrt(var + 1e-05) * gain[...] + shift[...]
        row = lax.broadcasted_iota(jnp.int32, (tile, 1), 0) + base
        norm = jnp.where(row < live[0], norm, 0.0)
        new = (latents.astype(FLOAT) + norm).astype(HALF)
        fresh[pl.ds(base, tile), :] = new
        pltpu.make_async_copy(
            fresh.at[pl.ds(base, tile), :], edge_new.at[pl.ds(base, tile), :], tile_out
        ).start()
        full = new.astype(FLOAT)
        messages[pl.ds(0, tile, stride=2), :] = full[:, :LANES]
        messages[pl.ds(1, tile, stride=2), :] = full[:, LANES:]

        def scatter(k, carry):
            first = k * UNROLL
            rows = [messages[pl.ds(2 * (first + u), 2), :] for u in range(UNROLL)]
            places = [pl.ds(receivers[base + first + u], 2) for u in range(UNROLL)]
            for start in range(0, UNROLL, COPIES):
                new_rows = [partial[u][places[start + u], :] + rows[start + u] for u in range(COPIES)]
                for u in range(COPIES):
                    partial[u][places[start + u], :] = new_rows[u]
            return carry

        def scatter_one(j, carry):
            rows = pl.ds(receivers[base + j], 2)
            partial[0][rows, :] = partial[0][rows, :] + messages[pl.ds(2 * j, 2), :]
            return carry

        count = jnp.clip(live[0] - base, 0, tile)
        whole = count // UNROLL
        lax.fori_loop(0, whole, scatter, 0)
        lax.fori_loop(whole * UNROLL, count, scatter_one, 0)
        return carry

    lax.fori_loop(0, steps, one_tile, 0)

    table_rows = sums.shape[0] // 2
    pieces = 3
    piece_rows = table_rows // pieces

    def total_chunk(k, carry):
        start = pl.multiple_of(k * CHUNK, CHUNK)
        for lanes in range(2):
            rows = pl.ds(2 * start + lanes, CHUNK, stride=2)
            total = partial[0][rows, :]
            for part in partial[1:]:
                total += part[rows, :]
            totals[pl.ds(lanes * table_rows + start, CHUNK), :] = total.astype(sums.dtype)
        return carry

    leaving = []
    for n in range(pieces):
        chunks = piece_rows // CHUNK
        lax.fori_loop(n * chunks, (n + 1) * chunks, total_chunk, 0)
        for lanes in range(2):
            rows = pl.ds(lanes * table_rows + n * piece_rows, piece_rows)
            leaving.append(pltpu.make_async_copy(totals.at[rows, :], sums.at[rows, :], sum_out.at[2 * n + lanes]))
            leaving[-1].start()
    for copy in leaving:
        copy.wait()
    pltpu.make_async_copy(fresh, edge_new, tile_out).wait()


def edge_block(senders, receivers, live, own, halo, edges, w_in, b_in, w_out, b_out, gain, shift):
    edge_rows, latent = edges.shape
    node_rows = own.shape[1]
    table_rows = node_rows + 2 * halo.shape[1]
    scratch = lambda rows: pltpu.VMEM((2 * rows, LANES), FLOAT)
    like = lambda array: pltpu.VMEM(array.shape, array.dtype)
    b_in, b_out, gain, shift = (v.reshape(1, latent) for v in (b_in, b_out, gain, shift))
    return pl.pallas_call(
        edge_kernel,
        in_specs=[pl.BlockSpec(memory_space=pltpu.SMEM)] + [ANY] * 6 + [VMEM] * 5,
        out_specs=[ANY] * 2,
        scratch_shapes=[
            pltpu.SMEM(senders.shape, senders.dtype), pltpu.SMEM(receivers.shape, receivers.dtype),
            like(own), like(halo), like(edges), like(w_in), like(edges), pltpu.VMEM((2 * table_rows, LANES), HALF),
            scratch(node_rows), scratch(table_rows), scratch(EDGE_TILE), scratch(EDGE_TILE),
            pltpu.SemaphoreType.DMA((6,)), pltpu.SemaphoreType.DMA, pltpu.SemaphoreType.DMA((6,)),
        ] + [scratch(table_rows)] * COPIES,
        out_shape=[
            jax.ShapeDtypeStruct((edge_rows, latent), HALF),
            jax.ShapeDtypeStruct((2 * table_rows, LANES), HALF),
        ],
        compiler_params=pltpu.CompilerParams(vmem_limit_bytes=VMEM_LIMIT),
        name="edges",
    )(live, senders, receivers, own, halo, edges, w_in, b_in, w_out, b_out, gain, shift)


def reverse_kernel(
    sums, own, rows_of, w_in, w_out, in_bias, out_bias, gain, shift,
    result,
    halo_in, own_in, halo_mine, own_mine, halo_out, own_out, halo_far, own_far, reduced, returned,
    pick, nodes, summed, fresh, vectors, all_in, all_out, all_vectors,
    part_send, part_recv, send, recv, local, halo_send, halo_recv, own_send, own_recv, row_send, row_recv,
    end_send, end_recv, end_local,
    *, parts, chans,
):
    dom = lax.axis_index("dom")
    chan = lax.axis_index("chan")
    side = chan // 2
    core = lax.rem(chan, 2)
    half = lax.rem(side + dom, 2)
    other = 1 - half
    far = lax.rem(chan + 2, chans)
    sibling = (dom, chan + 1 - 2 * core)
    across = (dom, far)
    latent, count = nodes.shape
    quarter = latent // chans
    halo_rows = reduced.shape[0]
    slots = halo_rows // parts
    table_rows = sums.shape[0] // 2

    def own_block(lanes, index):
        return sums.at[pl.ds(pl.multiple_of(lanes * table_rows + index * count, LANES), count), :]

    def halo_block(lanes, index):
        start = pl.multiple_of(lanes * table_rows + 2 * count + index * halo_rows, LANES)
        return sums.at[pl.ds(start, halo_rows), :]

    def describe(src, dst, sends, recvs, index, target):
        return pltpu.make_async_remote_copy(
            src_ref=src, dst_ref=dst, send_sem=sends.at[index], recv_sem=recvs.at[index],
            device_id=target, device_id_type=MESH,
        )

    def push(*where):
        copy = describe(*where)
        copy.start()
        return copy

    def fetch(src, dst, sems, index):
        copy = pltpu.make_async_copy(src, dst, sems.at[index])
        copy.start()
        return copy

    columns = pl.ds(pl.multiple_of(core * count, count), count)
    mine = [
        fetch(halo_block(other, core), halo_mine.at[other], local, 0),
        fetch(own_block(other, core), own_mine.at[other], local, 1),
        fetch(halo_block(half, core), halo_mine.at[half], local, 2),
        fetch(own_block(half, core), own_mine.at[half], local, 3),
    ]
    load = fetch(own.at[:, columns], nodes, local, 4)
    vectors[...] = jnp.zeros_like(vectors)
    for n, values in enumerate((in_bias, gain, shift)):
        vectors[n : n + 1, :quarter] = values[...].astype(FLOAT)
    enter(dom, chan, parts, chans)

    pair = [
        push(halo_block(other, 1 - core), halo_in.at[other], send, recv, 0, sibling),
        push(own_block(other, 1 - core), own_in.at[other], send, recv, 1, sibling),
        push(halo_block(half, 1 - core), halo_in.at[half], send, recv, 2, sibling),
        push(own_block(half, 1 - core), own_in.at[half], send, recv, 3, sibling),
    ]
    weights = [(w_in, all_in), (w_out, all_out), (vectors, all_vectors)]
    weight_crossed, weight_done = [], []
    for n, (src, dst) in enumerate(weights):
        weight_crossed.append(push(src, dst.at[chan], send, recv, 4 + 3 * n, across))
        weight_done.append(push(src, dst.at[chan], send, recv, 5 + 3 * n, sibling))
        dst[chan] = src[...]

    group_rows = halo_rows // GROUPS
    step_rows = count // STEPS
    mine[0].wait()
    pair[0].wait()
    halo_cross, own_cross = [], []
    for g in range(GROUPS):
        rows = pl.ds(g * group_rows, group_rows)
        halo_out[rows, :] = (
            halo_mine[other, rows, :].astype(FLOAT) + halo_in[other, rows, :].astype(FLOAT)
        ).astype(HALF)
        halo_cross.append(push(halo_out.at[rows, :], halo_far.at[rows, :], halo_send, halo_recv, g, across))
    mine[1].wait()
    pair[1].wait()
    for n in range(STEPS):
        rows = pl.ds(n * step_rows, step_rows)
        own_out[rows, :] = (
            own_mine[other, rows, :].astype(FLOAT) + own_in[other, rows, :].astype(FLOAT)
        ).astype(HALF)
        own_cross.append(push(own_out.at[rows, :], own_far.at[rows, :], own_send, own_recv, n, across))

    def send_part(k, carry):
        offset = offset_of(k, parts)
        rows = pl.ds(pl.multiple_of(k * slots, slots), slots)
        landing = pl.ds(pl.multiple_of(dom * slots, slots), slots)
        pltpu.make_async_remote_copy(
            src_ref=reduced.at[rows, :], dst_ref=returned.at[core, landing, :],
            send_sem=part_send, recv_sem=part_recv,
            device_id=(lax.rem(dom + parts - offset, parts), lax.rem(chan + 2 * (offset % 2), chans)),
            device_id_type=MESH,
        ).start()
        return carry

    mine[2].wait()
    pair[2].wait()
    group = parts // GROUPS
    for g in range(GROUPS):
        rows = pl.ds(g * group_rows, group_rows)
        halo_cross[g].wait()
        reduced[rows, :] = (
            halo_mine[half, rows, :].astype(FLOAT)
            + halo_in[half, rows, :].astype(FLOAT)
            + halo_far[rows, :].astype(FLOAT)
        ).astype(HALF)
        lax.fori_loop(g * group, min((g + 1) * group, parts - 1), send_part, 0)
    last = pl.ds((parts - 1) * slots, slots)
    landing = pl.ds(pl.multiple_of(dom * slots, slots), slots)
    pltpu.make_async_copy(reduced.at[last, :], returned.at[core, landing, :], part_recv).start()

    def choose(n, carry):
        start = pl.multiple_of(n * LANES, LANES)
        row = lax.broadcasted_iota(jnp.int32, (LANES, 1), 0) + (start + core * count)
        pick[pl.ds(start, LANES), :] = jnp.where(rows_of[...] == row, 1.0, 0.0).astype(HALF)
        return carry

    lax.fori_loop(0, count // LANES, choose, 0)

    for n, (src, dst) in enumerate(weights):
        weight_crossed[n].wait()
        weight_done.append(push(dst.at[far], dst.at[far], send, recv, 6 + 3 * n, sibling))
    mine[3].wait()
    pair[3].wait()

    arrived = returned.at[core]
    pltpu.make_async_copy(arrived, arrived, part_recv).wait()
    push(arrived, arrived, send, recv, 13, sibling).wait()

    values = returned[...].reshape(2 * halo_rows, LANES)
    sent = []
    for n in range(STEPS):
        rows = pl.ds(n * step_rows, step_rows)
        total = jnp.dot(pick[rows, :], values, preferred_element_type=FLOAT)
        total += own_mine[half, rows, :].astype(FLOAT) + own_in[half, rows, :].astype(FLOAT)
        own_cross[n].wait()
        summed[half, rows, :] = (total + own_far[rows, :].astype(FLOAT)).astype(HALF)
        piece = summed.at[half, rows, :]
        sent.append(push(piece, piece, row_send, row_recv, n, across))

    load.wait()
    for copy in weight_done:
        copy.wait()
    first_layer = all_in[...].reshape(latent, 2 * latent)
    second_layer = all_out[...].reshape(latent, latent)
    column = jnp.concatenate([all_vectors[c].T[:quarter, :] for c in range(chans)], axis=0)
    bias = jnp.concatenate(
        [jnp.broadcast_to(out_bias[:, n : n + LANES], (8, LANES)).T for n in range(0, latent, LANES)], axis=0
    )
    both = (((1,), (1,)), ((), ()))
    final = []
    for n in range(STEPS):
        rows = pl.ds(n * step_rows, step_rows)
        latents = nodes[:, rows]
        pre = jnp.dot(first_layer[:, :latent], latents, preferred_element_type=FLOAT)
        piece = summed.at[other, rows, :]
        describe(piece, piece, row_send, row_recv, n, across).wait_recv()
        total = jnp.concatenate([summed[0, rows, :], summed[1, rows, :]], axis=1)
        pre += lax.dot_general(first_layer[:, latent:], total, both, preferred_element_type=FLOAT)
        hidden = silu_rows(pre + column[:, 0:1]).astype(HALF)
        post = lax.dot_general(
            second_layer, hidden, (((0,), (0,)), ((), ())), preferred_element_type=FLOAT
        ) + bias[:, 0:1]
        centred = post - jnp.mean(post, axis=0, keepdims=True)
        var = jnp.mean(centred * centred, axis=0, keepdims=True)
        norm = centred * lax.rsqrt(var + 1e-05) * column[:, 1:2] + column[:, 2:3]
        new = (latents.astype(FLOAT) + norm).astype(HALF)
        for c in range(chans):
            fresh[c, :, rows] = new[c * quarter : (c + 1) * quarter, :]
        place = pl.ds(pl.multiple_of(core * count + n * step_rows, step_rows), step_rows)
        final.append(fetch(fresh.at[chan, :, rows], result.at[:, place], end_local, n))
        final.append(
            push(fresh.at[chan + 1 - 2 * core, :, rows], result.at[:, place], end_send, end_recv, n, sibling)
        )

    for copy in sent:
        copy.wait_send()
    gone = reduced.at[pl.ds(0, (parts - 1) * slots), :]
    pltpu.make_async_copy(gone, gone, part_send).wait()
    for copy in final:
        copy.wait()


def reverse(sums, own, rows_of, w_in, w_out, in_bias, out_bias, gain, shift, parts, chans):
    latent, node_rows = own.shape
    count = node_rows // 2
    halo_rows = (sums.shape[0] - 2 * node_rows) // 4
    half = lambda *shape: pltpu.VMEM(shape, HALF)
    dma = lambda count: pltpu.SemaphoreType.DMA((count,))
    return pl.pallas_call(
        functools.partial(reverse_kernel, parts=parts, chans=chans),
        in_specs=[ANY, ANY] + [VMEM] * 7,
        out_specs=VMEM,
        out_shape=jax.ShapeDtypeStruct((latent // chans, node_rows), HALF),
        scratch_shapes=[
            half(2, halo_rows, LANES), half(2, count, LANES),
            half(2, halo_rows, LANES), half(2, count, LANES),
            half(halo_rows, LANES), half(count, LANES),
            half(halo_rows, LANES), half(count, LANES),
            half(halo_rows, LANES), half(2, halo_rows, LANES),
            half(count, 2 * halo_rows), half(latent, count), half(2, count, LANES),
            half(chans, latent // chans, count), pltpu.VMEM((8, LANES), FLOAT),
            half(chans, *w_in.shape), half(chans, *w_out.shape), pltpu.VMEM((chans, 8, LANES), FLOAT),
            pltpu.SemaphoreType.DMA,
            pltpu.SemaphoreType.DMA,
            dma(14), dma(14), dma(5), dma(GROUPS), dma(GROUPS), dma(STEPS), dma(STEPS), dma(STEPS), dma(STEPS),
            dma(STEPS), dma(STEPS), dma(STEPS),
        ],
        compiler_params=pltpu.CompilerParams(
            collective_id=1, has_side_effects=True, vmem_limit_bytes=VMEM_LIMIT
        ),
        name="reverse",
    )(sums, own, rows_of, w_in, w_out, in_bias, out_bias, gain, shift)


def body(
    node_latent,
    edge_latent,
    senders,
    receivers,
    edge_count,
    send_list,
    w_edge_in,
    edge_in_bias,
    w_edge_out,
    edge_out_bias,
    edge_gain,
    edge_shift,
    w_node_in,
    node_in_bias,
    w_node_out,
    node_out_bias,
    node_gain,
    node_shift,
):
    node_rows, quarter = node_latent.shape
    parts = lax.axis_size("dom")
    chans = lax.axis_size("chan")
    chan = lax.axis_index("chan")
    slots = send_list.shape[2]
    edge_rows = edge_latent.shape[0]

    own, halo, sender_rows, receiver_rows = forward(
        send_list[0].T, node_latent.T, senders.reshape(-1, LANES), receivers.reshape(-1, LANES), parts, chans
    )
    live = jnp.clip(edge_count - chan * edge_rows, 0, edge_rows)
    edge_new, sums = edge_block(
        sender_rows.reshape(-1), receiver_rows.reshape(-1), live, own, halo, edge_latent, w_edge_in,
        edge_in_bias, w_edge_out, edge_out_bias, edge_gain, edge_shift,
    )

    rows_of = send_list[0].reshape(parts, 2, slots // 2).transpose(1, 0, 2).reshape(1, parts * slots)
    row = lambda vector: vector.reshape(1, -1)
    node_new = reverse(
        sums, own, rows_of, w_node_in.T, w_node_out, row(node_in_bias), row(node_out_bias),
        row(node_gain), row(node_shift), parts, chans,
    )
    return (node_new.T, edge_new)


def solution(mesh):
    placed = (
        P("dom", "chan"),
        P(("dom", "chan"), None),
        P(("dom", "chan")),
        P(("dom", "chan")),
        P("dom"),
        P("dom", None, None),
        P(),
        P(),
        P(),
        P(),
        P(),
        P(),
        P(None, "chan"),
        P("chan"),
        P("chan", None),
        P(),
        P("chan"),
        P("chan"),
    )
    return jax.shard_map(
        body,
        mesh=mesh,
        in_specs=placed,
        out_specs=(P("dom", "chan"), P(("dom", "chan"), None)),
        check_vma=False,
    )
```

time: 107 us -> 97.1 us (0.907)
  Pallas kernels: 101 us -> 93 us
  local copies, waits for them, and re-layouts: 4.09 us -> 2.5 us
    pallas_call x1, Pallas kernels: 39.9 us -> 36.6 us  [reverse(): pl.pallas_call(functools.partial(reverse_kernel, parts=parts, chans=chans...]
    pallas_call x1, Pallas kernels: 28.7 us -> 25.9 us  [edge_block(): pl.pallas_call(edge_kernel, in_specs=[pl.BlockSpec(memory_space=pltpu.SME...]
    pallas_call x1, Pallas kernels: 32.3 us -> 30.6 us  [forward(): pl.pallas_call(functools.partial(forward_kernel, parts=parts, chans=chans...]
where the time goes in v4:
time: 97.1 us; the launch traced here: 96.9 us
  Pallas kernels  93 us (96%)
  local copies, waits for them, and re-layouts  2.5 us (3%)
  between operations  1.33 us (1%)
    pallas_call x1, Pallas kernels, reverse(): pl.pallas_call(functools.partial(reverse_kernel, parts=parts, chans=chans...  36.6 us
    pallas_call x1, Pallas kernels, forward(): pl.pallas_call(functools.partial(forward_kernel, parts=parts, chans=chans...  30.6 us
    pallas_call x1, Pallas kernels, edge_block(): pl.pallas_call(edge_kernel, in_specs=[pl.BlockSpec(memory_space=pltpu.SME...  25.9 us

profile of v4, /device:TPU:1, one launch (start us, length us, event | category | flops | bytes accessed | tf_op | source)
XLA Modules:
  0.0 96.9 jit_solution(2575939956335143226)
XLA Ops:
  0.6 30.6 %forward.1 = (bf16[256,2560]{1,0:T(8,128)(2,1)}, bf16[4,1024,128]{2,1,0:T(8,128)(2,1)}, s32[42,128]{1,0:T(8,128)}, s32[42,128]{1,0:T(8,128)}) custom-call(s32[32,64]{1,0:T(8,128)} %bitcast.25, bf16[64,2560]{1,0:T(8,128)(2,1)} %bitcast.22, s32[42,128]{1,0:T(8,128)} %bitcast.29, s32[42,128]{1,0:T(8,128)} %bitcast.30), custom_call_target="tpu_custom_call" | custom-call | tf_op jit(solution)/shard_map/forward/pallas_call | solution.py:177
  31.8 0.0 copy-start
  31.9 25.9 %edges.1 = (bf16[5376,256]{1,0:T(8,128)(2,1)}, bf16[9216,128]{1,0:T(8,128)(2,1)}) custom-call(s32[1]{0:T(128)S(6)} %min.6.live, s32[5376]{0:T(1024)} %bitcast.27, s32[5376]{0:T(1024)} %bitcast.28, bf16[256,2560]{1,0:T(8,128)(2,1)} %get-tuple-element.10.own_in.own, bf16[4,1024,128]{2,1,0:T(8,128)(2,1)} %get-tuple-element.11.halo_in, ...), custom_call_target="tpu_custom_call" | custom-call | tf_op jit(solution)/shard_map/edges/pallas_call | solution.py:353
  57.8 0.0 copy-done
  57.8 0.1 copy.21
  57.8 0.7 reshape.51.rows_of
  58.5 36.6 %reverse.1 = bf16[64,2560]{1,0:T(8,128)(2,1)} custom-call(bf16[9216,128]{1,0:T(8,128)(2,1)} %get-tuple-element.12.sums, bf16[256,2560]{1,0:T(8,128)(2,1)} %get-tuple-element.10.own_in.own, s32[1,2048]{1,0:T(1,128)} %reshape.51.rows_of, bf16[64,512]{1,0:T(8,128)(2,1)} %bitcast.24, bf16[64,256]{1,0:T(8,128)(2,1)} %w_out.3, bf16[1,64]{1,0:T(2,128)(2,1)} %bitcast.36, ...), custom_call_target="tpu_custom_call" | custom-call | tf_op jit(solution)/shard_map/reverse/pallas_call | solution.py:571
  95.1 1.7 %copy.24 = bf16[2560,64]{0,1:T(8,128)(2,1)} copy(bf16[2560,64]{0,1:T(8,128)(2,1)} %bitcast.21) | data formatting | bytes 655360
Async XLA Ops:
  31.8 25.9 %copy-start = (s32[1,64,32]{1,2,0:T(8,128)S(1)}, s32[1,64,32]{1,2,0:T(8,128)}, u32[]{:S(2)}) copy-start(s32[1,64,32]{1,2,0:T(8,128)} %param.23) | copy-start | bytes 24580

commit v5 on v4

--- a/solution.py
+++ b/solution.py
@@ -8,9 +8,9 @@
 from jax.sharding import PartitionSpec as P
 
 LANES = 128
-EDGE_TILE = 1344
-UNROLL = 32
+EDGE_TILE = 128
 COPIES = 4
+GATHER = 16
 CHUNK = 512
 GROUPS = 4
 STEPS = 5
@@ -49,7 +49,7 @@
 
 
 def forward_kernel(
-    send_rows, nodes, senders, receivers,
+    send_rows, live, nodes, senders, receivers,
     own, halo, sender_rows, receiver_rows,
     wide, stage, outgoing, part_send, part_recv, send, recv, local,
     *, parts, chans,
@@ -145,7 +145,9 @@
     offset = (dom + 2 * parts - 1 - (slot >> 5)) & (parts - 1)
     place = (offset >> 1) + half * (offset & 1)
     halo_row = node_rows + ((slot >> 4) & 1) * (parts * slots) + place * slots + (slot & 15)
-    receiver_rows[...] = 2 * jnp.where(index < node_rows, index, halo_row)
+    index = jnp.where(index < node_rows, index, halo_row)
+    edge = LANES * lax.broadcasted_iota(jnp.int32, index.shape, 0) + lax.broadcasted_iota(jnp.int32, index.shape, 1)
+    receiver_rows[...] = 2 * jnp.where(edge < live[0], index, node_rows + 2 * parts * slots)
 
     for g in range(GROUPS):
         share(g)
@@ -169,14 +171,14 @@
     pltpu.make_async_copy(sent, sent, part_send).wait()
 
 
-def forward(send_rows, nodes, senders, receivers, parts, chans):
+def forward(send_rows, live, nodes, senders, receivers, parts, chans):
     quarter, node_rows = nodes.shape
     slots = send_rows.shape[0]
     rows = parts * slots // 2
     copies = 3 * (STEPS + GROUPS)
     return pl.pallas_call(
         functools.partial(forward_kernel, parts=parts, chans=chans),
-        in_specs=[pl.BlockSpec(memory_space=pltpu.SMEM)] + [VMEM] * 3,
+        in_specs=[pl.BlockSpec(memory_space=pltpu.SMEM)] * 2 + [VMEM] * 3,
         out_specs=[ANY] * 2 + [VMEM] * 2,
         out_shape=[
             jax.ShapeDtypeStruct((chans * quarter, node_rows), HALF),
@@ -198,16 +200,18 @@
             collective_id=0, has_side_effects=True, vmem_limit_bytes=VMEM_LIMIT
         ),
         name="forward",
-    )(send_rows, nodes, senders, receivers)
+    )(send_rows, live, nodes, senders, receivers)
 
 
 def edge_kernel(
     live, senders_in, receivers_in, own_in, halo_in, edges_in, w_in_in, b_in, w_out, b_out, gain, shift,
     edge_new, sums,
-    senders, receivers, own, halo, edges, w_in, fresh, totals, sent, received, gathered, messages, loads, tile_out, sum_out,
+    senders, receivers, own, halo, edges, w_in, fresh, totals, sent, received, gathered0, gathered1, messages0, messages1, loads, tile_out, sum_out,
     *partial,
 ):
-    tile = messages.shape[0] // 2
+    gathered = (gathered0, gathered1)
+    messages = (messages0, messages1)
+    tile = messages0.shape[0] // 2
     edge_rows, latent = edges.shape
     node_rows = own.shape[1]
     chans, halo_rows, _ = halo.shape
@@ -257,26 +261,28 @@
     for copy in loading[3:]:
         copy.wait()
 
-    def one_tile(step, carry):
-        base = pl.multiple_of(step * tile, tile)
-
-        def gather(k, carry):
-            first = k * UNROLL
+    def gather(base, target):
+        for first in range(0, tile, GATHER):
             rows = []
-            for u in range(UNROLL):
-                s = senders[base + first + u]
-                r = receivers[base + first + u]
-                rows.append(sent[pl.ds(s, 2), :] + received[pl.ds(r, 2), :])
-            for u in range(UNROLL):
-                gathered[pl.ds(2 * (first + u), 2), :] = rows[u]
-            return carry
-
-        lax.fori_loop(0, tile // UNROLL, gather, 0)
-
+            for u in range(first, first + GATHER):
+                rows.append(sent[pl.ds(senders[base + u], 2), :] + received[pl.ds(receivers[base + u], 2), :])
+            for u in range(GATHER):
+                target[2 * (first + u) : 2 * (first + u) + 2, :] = rows[u]
+
+    def scatter(base, source):
+        for first in range(0, tile, COPIES):
+            places = [pl.ds(receivers[base + first + u], 2) for u in range(COPIES)]
+            new_rows = [
+                partial[u][places[u], :] + source[2 * (first + u) : 2 * (first + u) + 2, :] for u in range(COPIES)
+            ]
+            for u in range(COPIES):
+                partial[u][places[u], :] = new_rows[u]
+
+    def dense(base, source, target):
         latents = edges[pl.ds(base, tile), :]
         pre = jnp.dot(latents, w_in[:latent, :], preferred_element_type=FLOAT)
-        low = pre[:, :LANES] + gathered[pl.ds(0, tile, stride=2), :]
-        high = pre[:, LANES:] + gathered[pl.ds(1, tile, stride=2), :]
+        low = pre[:, :LANES] + source[pl.ds(0, tile, stride=2), :]
+        high = pre[:, LANES:] + source[pl.ds(1, tile, stride=2), :]
         hidden = silu_rows(jnp.concatenate([low, high], axis=1) + b_in[...]).astype(HALF)
         post = jnp.dot(hidden, w_out[...], preferred_element_type=FLOAT) + b_out[...]
         centred = post - jnp.mean(post, axis=-1, keepdims=True)
@@ -286,35 +292,25 @@
         norm = jnp.where(row < live[0], norm, 0.0)
         new = (latents.astype(FLOAT) + norm).astype(HALF)
         fresh[pl.ds(base, tile), :] = new
-        pltpu.make_async_copy(
-            fresh.at[pl.ds(base, tile), :], edge_new.at[pl.ds(base, tile), :], tile_out
-        ).start()
         full = new.astype(FLOAT)
-        messages[pl.ds(0, tile, stride=2), :] = full[:, :LANES]
-        messages[pl.ds(1, tile, stride=2), :] = full[:, LANES:]
-
-        def scatter(k, carry):
-            first = k * UNROLL
-            rows = [messages[pl.ds(2 * (first + u), 2), :] for u in range(UNROLL)]
-            places = [pl.ds(receivers[base + first + u], 2) for u in range(UNROLL)]
-            for start in range(0, UNROLL, COPIES):
-                new_rows = [partial[u][places[start + u], :] + rows[start + u] for u in range(COPIES)]
-                for u in range(COPIES):
-                    partial[u][places[start + u], :] = new_rows[u]
-            return carry
-
-        def scatter_one(j, carry):
-            rows = pl.ds(receivers[base + j], 2)
-            partial[0][rows, :] = partial[0][rows, :] + messages[pl.ds(2 * j, 2), :]
-            return carry
-
-        count = jnp.clip(live[0] - base, 0, tile)
-        whole = count // UNROLL
-        lax.fori_loop(0, whole, scatter, 0)
-        lax.fori_loop(whole * UNROLL, count, scatter_one, 0)
+        target[pl.ds(0, tile, stride=2), :] = full[:, :LANES]
+        target[pl.ds(1, tile, stride=2), :] = full[:, LANES:]
+
+    def two_tiles(k, carry):
+        for p in range(2):
+            step = 2 * k + p
+            base = pl.multiple_of(step * tile, tile)
+            gather(jnp.minimum(step + 1, steps - 1) * tile, gathered[1 - p])
+            dense(base, gathered[p], messages[p])
+            scatter(jnp.maximum(step - 1, 0) * tile, messages[1 - p])
+        rows = pl.ds(pl.multiple_of(2 * k * tile, 2 * tile), 2 * tile)
+        pltpu.make_async_copy(fresh.at[rows, :], edge_new.at[rows, :], tile_out).start()
         return carry
 
-    lax.fori_loop(0, steps, one_tile, 0)
+    messages1[...] = jnp.zeros_like(messages1)
+    gather(0, gathered0)
+    lax.fori_loop(0, steps // 2, two_tiles, 0)
+    scatter((steps - 1) * tile, messages1)
 
     table_rows = sums.shape[0] // 2
     pieces = 3
@@ -357,9 +353,9 @@
         scratch_shapes=[
             pltpu.SMEM(senders.shape, senders.dtype), pltpu.SMEM(receivers.shape, receivers.dtype),
             like(own), like(halo), like(edges), like(w_in), like(edges), pltpu.VMEM((2 * table_rows, LANES), HALF),
-            scratch(node_rows), scratch(table_rows), scratch(EDGE_TILE), scratch(EDGE_TILE),
+            scratch(node_rows), scratch(table_rows + 4), *[scratch(EDGE_TILE)] * 4,
             pltpu.SemaphoreType.DMA((6,)), pltpu.SemaphoreType.DMA, pltpu.SemaphoreType.DMA((6,)),
-        ] + [scratch(table_rows)] * COPIES,
+        ] + [scratch(table_rows + 4)] * COPIES,
         out_shape=[
             jax.ShapeDtypeStruct((edge_rows, latent), HALF),
             jax.ShapeDtypeStruct((2 * table_rows, LANES), HALF),
@@ -588,7 +584,7 @@
             dma(STEPS), dma(STEPS), dma(STEPS),
         ],
         compiler_params=pltpu.CompilerParams(
-            collective_id=1, has_side_effects=True, vmem_limit_bytes=VMEM_LIMIT
+            collective_id=1, has_side_effects=True, vmem_limit_bytes=53 * 2**20
         ),
         name="reverse",
     )(sums, own, rows_of, w_in, w_out, in_bias, out_bias, gain, shift)
@@ -621,10 +617,10 @@
     slots = send_list.shape[2]
     edge_rows = edge_latent.shape[0]
 
+    live = jnp.clip(edge_count - chan * edge_rows, 0, edge_rows)
     own, halo, sender_rows, receiver_rows = forward(
-        send_list[0].T, node_latent.T, senders.reshape(-1, LANES), receivers.reshape(-1, LANES), parts, chans
+        send_list[0].T, live, node_latent.T, senders.reshape(-1, LANES), receivers.reshape(-1, LANES), parts, chans
     )
-    live = jnp.clip(edge_count - chan * edge_rows, 0, edge_rows)
     edge_new, sums = edge_block(
         sender_rows.reshape(-1), receiver_rows.reshape(-1), live, own, halo, edge_latent, w_edge_in,
         edge_in_bias, w_edge_out, edge_out_bias, edge_gain, edge_shift,

time: 97.1 us -> 95 us (0.978)
  local copies, waits for them, and re-layouts: 2.5 us -> 0.95 us
    pallas_call x1, Pallas kernels: 25.9 us -> 24.5 us  [edge_block(): pl.pallas_call(edge_kernel, in_specs=[pl.BlockSpec(memory_space=pltpu.SME...]
where the time goes in v5:
time: 95 us; the launch traced here: 94.8 us
  Pallas kernels  92.5 us (97%)
  between operations  1.42 us (1%)
    pallas_call x1, Pallas kernels, reverse(): pl.pallas_call(functools.partial(reverse_kernel, parts=parts, chans=chans...  37.4 us
    pallas_call x1, Pallas kernels, forward(): pl.pallas_call(functools.partial(forward_kernel, parts=parts, chans=chans...  30.6 us
    pallas_call x1, Pallas kernels, edge_block(): pl.pallas_call(edge_kernel, in_specs=[pl.BlockSpec(memory_space=pltpu.SME...  24.5 us

profile of v5, /device:TPU:1, one launch (start us, length us, event | category | flops | bytes accessed | tf_op | source)
XLA Modules:
  0.0 94.8 jit_solution(8802465884353483480)
XLA Ops:
  1.3 30.6 %forward.1 = (bf16[256,2560]{1,0:T(8,128)(2,1)}, bf16[4,1024,128]{2,1,0:T(8,128)(2,1)}, s32[42,128]{1,0:T(8,128)}, s32[42,128]{1,0:T(8,128)}) custom-call(s32[32,64]{1,0:T(8,128)} %bitcast.29, s32[1]{0:T(128)S(6)} %min.6.live, bf16[64,2560]{1,0:T(8,128)(2,1)} %bitcast.27, s32[42,128]{1,0:T(8,128)} %bitcast.33, s32[42,128]{1,0:T(8,128)} %bitcast.34), custom_call_target="tpu_custom_call" | custom-call | tf_op jit(solution)/shard_map/forward/pallas_call | solution.py:179
  31.8 0.0 copy-start.6
  31.9 0.0 copy-start
  31.9 0.0 copy-start.1
  31.9 0.0 copy-start.2
  31.9 0.0 copy-start.3
  31.9 0.0 copy-start.4
  31.9 0.0 copy-start.5
  31.9 24.5 %edges.1 = (bf16[5376,256]{1,0:T(8,128)(2,1)}, bf16[9216,128]{1,0:T(8,128)(2,1)}) custom-call(s32[1]{0:T(128)S(6)} %min.6.live, s32[5376]{0:T(1024)} %bitcast.31, s32[5376]{0:T(1024)} %bitcast.32, bf16[256,2560]{1,0:T(8,128)(2,1)} %get-tuple-element.10.own_in.own, bf16[4,1024,128]{2,1,0:T(8,128)(2,1)} %get-tuple-element.11.halo_in, ...), custom_call_target="tpu_custom_call" | custom-call | tf_op jit(solution)/shard_map/edges/pallas_call | solution.py:349
  56.5 0.0 copy-done.6
  56.5 0.1 copy.21
  56.6 0.1 reshape.51.rows_of
  56.6 0.0 copy-done
  56.7 0.0 copy-done.1
  56.7 0.0 copy-done.2
  56.7 0.0 copy-done.3
  56.7 0.0 copy-done.4
  56.7 0.0 copy-done.5
  56.7 37.4 %reverse.1 = bf16[64,2560]{1,0:T(8,128)(2,1)S(1)} custom-call(bf16[9216,128]{1,0:T(8,128)(2,1)} %get-tuple-element.12.sums, bf16[256,2560]{1,0:T(8,128)(2,1)} %get-tuple-element.10.own_in.own, s32[1,2048]{1,0:T(1,128)S(1)} %reshape.51.rows_of, bf16[64,512]{1,0:T(8,128)(2,1)S(1)} %bitcast.22, bf16[64,256]{1,0:T(8,128)(2,1)S(1)} %copy-done.1, ...), custom_call_target="tpu_custom_call" | custom-call | tf_op jit(solution)/shard_map/reverse/pallas_call | solution.py:567
  94.1 0.7 copy.24
Async XLA Ops:
  31.8 24.6 %copy-start.6 = (s32[1,64,32]{1,2,0:T(8,128)S(1)}, s32[1,64,32]{1,2,0:T(8,128)}, u32[]{:S(2)}) copy-start(s32[1,64,32]{1,2,0:T(8,128)} %param.23) | copy-start | bytes 24580
  31.9 24.8 %copy-start = (bf16[512,64]{0,1:T(8,128)(2,1)S(1)}, bf16[512,64]{0,1:T(8,128)(2,1)}, u32[]{:S(2)}) copy-start(bf16[512,64]{0,1:T(8,128)(2,1)} %param.30) | copy-start | bytes 196612
  31.9 24.8 %copy-start.1 = (bf16[64,256]{1,0:T(8,128)(2,1)S(1)}, bf16[64,256]{1,0:T(8,128)(2,1)}, u32[]{:S(2)}) copy-start(bf16[64,256]{1,0:T(8,128)(2,1)} %w_out.3) | copy-start | bytes 98308
  31.9 24.8 %copy-start.2 = (f32[256]{0:T(256)S(1)}, f32[256]{0:T(256)}, u32[]{:S(2)}) copy-start(f32[256]{0:T(256)} %param.33) | copy-start | bytes 3076
  31.9 24.8 %copy-start.3 = (bf16[64]{0:T(256)(128)(2,1)S(1)}, bf16[64]{0:T(256)(128)(2,1)}, u32[]{:S(2)}) copy-start(bf16[64]{0:T(256)(128)(2,1)} %param.31) | copy-start | bytes 388
  31.9 24.8 %copy-start.4 = (f32[64]{0:T(128)S(1)}, f32[64]{0:T(128)}, u32[]{:S(2)}) copy-start(f32[64]{0:T(128)} %param.34) | copy-start | bytes 772
  31.9 24.8 %copy-start.5 = (f32[64]{0:T(128)S(1)}, f32[64]{0:T(128)}, u32[]{:S(2)}) copy-start(f32[64]{0:T(128)} %param.35) | copy-start | bytes 772

commit v6 on v5

--- a/solution.py
+++ b/solution.py
@@ -8,8 +8,8 @@
 from jax.sharding import PartitionSpec as P
 
 LANES = 128
-EDGE_TILE = 128
-COPIES = 4
+EDGE_TILE = 192
+COPIES = 6
 GATHER = 16
 CHUNK = 512
 GROUPS = 4
@@ -147,7 +147,8 @@
     halo_row = node_rows + ((slot >> 4) & 1) * (parts * slots) + place * slots + (slot & 15)
     index = jnp.where(index < node_rows, index, halo_row)
     edge = LANES * lax.broadcasted_iota(jnp.int32, index.shape, 0) + lax.broadcasted_iota(jnp.int32, index.shape, 1)
-    receiver_rows[...] = 2 * jnp.where(edge < live[0], index, node_rows + 2 * parts * slots)
+    left_over = live[0] - chan * senders.shape[0] * LANES
+    receiver_rows[...] = 2 * jnp.where(edge < left_over, index, node_rows + 2 * parts * slots)
 
     for g in range(GROUPS):
         share(g)
@@ -217,6 +218,7 @@
     chans, halo_rows, _ = halo.shape
     quarter = latent // chans
     steps = edge_rows // tile
+    count = live[0] - lax.axis_index("chan") * edge_rows
 
     loading = []
     for n, (src, dst) in enumerate((
@@ -289,7 +291,7 @@
         var = jnp.mean(centred * centred, axis=-1, keepdims=True)
         norm = centred * lax.rsqrt(var + 1e-05) * gain[...] + shift[...]
         row = lax.broadcasted_iota(jnp.int32, (tile, 1), 0) + base
-        norm = jnp.where(row < live[0], norm, 0.0)
+        norm = jnp.where(row < count, norm, 0.0)
         new = (latents.astype(FLOAT) + norm).astype(HALF)
         fresh[pl.ds(base, tile), :] = new
         full = new.astype(FLOAT)
@@ -613,16 +615,13 @@
     node_rows, quarter = node_latent.shape
     parts = lax.axis_size("dom")
     chans = lax.axis_size("chan")
-    chan = lax.axis_index("chan")
     slots = send_list.shape[2]
-    edge_rows = edge_latent.shape[0]
-
-    live = jnp.clip(edge_count - chan * edge_rows, 0, edge_rows)
+
     own, halo, sender_rows, receiver_rows = forward(
-        send_list[0].T, live, node_latent.T, senders.reshape(-1, LANES), receivers.reshape(-1, LANES), parts, chans
+        send_list[0].T, edge_count, node_latent.T, senders.reshape(-1, LANES), receivers.reshape(-1, LANES), parts, chans
     )
     edge_new, sums = edge_block(
-        sender_rows.reshape(-1), receiver_rows.reshape(-1), live, own, halo, edge_latent, w_edge_in,
+        sender_rows.reshape(-1), receiver_rows.reshape(-1), edge_count, own, halo, edge_latent, w_edge_in,
         edge_in_bias, w_edge_out, edge_out_bias, edge_gain, edge_shift,
     )
 

time: 95 us -> 92.4 us (0.973)
  Pallas kernels: 92.5 us -> 90.1 us
    pallas_call x1, Pallas kernels: 24.5 us -> 22.6 us  [edge_block(): pl.pallas_call(edge_kernel, in_specs=[pl.BlockSpec(memory_space=pltpu.SME...]
where the time goes in v6:
time: 92.4 us
  Pallas kernels  90.1 us (98%)
  between operations  1.42 us (2%)
  local copies, waits for them, and re-layouts  0.95 us (1%)
    pallas_call x1, Pallas kernels, reverse(): pl.pallas_call(functools.partial(reverse_kernel, parts=parts, chans=chans...  36.9 us
    pallas_call x1, Pallas kernels, forward(): pl.pallas_call(functools.partial(forward_kernel, parts=parts, chans=chans...  30.6 us
    pallas_call x1, Pallas kernels, edge_block(): pl.pallas_call(edge_kernel, in_specs=[pl.BlockSpec(memory_space=pltpu.SME...  22.6 us

profile of v6, /device:TPU:1, one launch (start us, length us, event | category | flops | bytes accessed | tf_op | source)
XLA Modules:
  0.0 92.4 jit_solution(17348317002995055073)
XLA Ops:
  1.3 30.6 %forward.1 = (bf16[256,2560]{1,0:T(8,128)(2,1)}, bf16[4,1024,128]{2,1,0:T(8,128)(2,1)}, s32[42,128]{1,0:T(8,128)}, s32[42,128]{1,0:T(8,128)}) custom-call(s32[32,64]{1,0:T(8,128)} %bitcast.28, s32[1]{0:T(128)S(6)} %copy.23.live, bf16[64,2560]{1,0:T(8,128)(2,1)} %bitcast.26, s32[42,128]{1,0:T(8,128)} %bitcast.32, s32[42,128]{1,0:T(8,128)} %bitcast.33), custom_call_target="tpu_custom_call" | custom-call | tf_op jit(solution)/shard_map/forward/pallas_call | solution.py:180
  31.8 0.0 copy-start.6
  31.9 0.0 copy-start
  31.9 0.0 copy-start.1
  31.9 0.0 copy-start.2
  31.9 0.0 copy-start.3
  31.9 0.0 copy-start.4
  31.9 0.0 copy-start.5
  31.9 22.6 %edges.1 = (bf16[5376,256]{1,0:T(8,128)(2,1)}, bf16[9216,128]{1,0:T(8,128)(2,1)}) custom-call(s32[1]{0:T(128)S(6)} %copy.23.live, s32[5376]{0:T(1024)} %bitcast.30, s32[5376]{0:T(1024)} %bitcast.31, bf16[256,2560]{1,0:T(8,128)(2,1)} %get-tuple-element.10.own_in.own, bf16[4,1024,128]{2,1,0:T(8,128)(2,1)} %get-tuple-element.11.halo_in, ...), custom_call_target="tpu_custom_call" | custom-call | tf_op jit(solution)/shard_map/edges/pallas_call | solution.py:351
  54.6 0.0 copy-done.6
  54.6 0.1 copy.21
  54.6 0.1 reshape.51.rows_of
  54.7 0.0 copy-done
  54.8 0.0 copy-done.1
  54.8 0.0 copy-done.2
  54.8 0.0 copy-done.3
  54.8 0.0 copy-done.4
  54.8 0.0 copy-done.5
  54.8 36.9 %reverse.1 = bf16[64,2560]{1,0:T(8,128)(2,1)S(1)} custom-call(bf16[9216,128]{1,0:T(8,128)(2,1)} %get-tuple-element.12.sums, bf16[256,2560]{1,0:T(8,128)(2,1)} %get-tuple-element.10.own_in.own, s32[1,2048]{1,0:T(1,128)S(1)} %reshape.51.rows_of, bf16[64,512]{1,0:T(8,128)(2,1)S(1)} %bitcast.21, bf16[64,256]{1,0:T(8,128)(2,1)S(1)} %copy-done.1, ...), custom_call_target="tpu_custom_call" | custom-call | tf_op jit(solution)/shard_map/reverse/pallas_call | solution.py:569
  91.7 0.7 copy.24
Async XLA Ops:
  31.8 22.7 %copy-start.6 = (s32[1,64,32]{1,2,0:T(8,128)S(1)}, s32[1,64,32]{1,2,0:T(8,128)}, u32[]{:S(2)}) copy-start(s32[1,64,32]{1,2,0:T(8,128)} %param.23) | copy-start | bytes 24580
  31.9 22.9 %copy-start = (bf16[512,64]{0,1:T(8,128)(2,1)S(1)}, bf16[512,64]{0,1:T(8,128)(2,1)}, u32[]{:S(2)}) copy-start(bf16[512,64]{0,1:T(8,128)(2,1)} %param.30) | copy-start | bytes 196612
  31.9 22.9 %copy-start.1 = (bf16[64,256]{1,0:T(8,128)(2,1)S(1)}, bf16[64,256]{1,0:T(8,128)(2,1)}, u32[]{:S(2)}) copy-start(bf16[64,256]{1,0:T(8,128)(2,1)} %w_out.3) | copy-start | bytes 98308
  31.9 22.9 %copy-start.2 = (f32[256]{0:T(256)S(1)}, f32[256]{0:T(256)}, u32[]{:S(2)}) copy-start(f32[256]{0:T(256)} %param.33) | copy-start | bytes 3076
  31.9 22.9 %copy-start.3 = (bf16[64]{0:T(256)(128)(2,1)S(1)}, bf16[64]{0:T(256)(128)(2,1)}, u32[]{:S(2)}) copy-start(bf16[64]{0:T(256)(128)(2,1)} %param.31) | copy-start | bytes 388
  31.9 22.9 %copy-start.4 = (f32[64]{0:T(128)S(1)}, f32[64]{0:T(128)}, u32[]{:S(2)}) copy-start(f32[64]{0:T(128)} %param.34) | copy-start | bytes 772
  31.9 22.9 %copy-start.5 = (f32[64]{0:T(128)S(1)}, f32[64]{0:T(128)}, u32[]{:S(2)}) copy-start(f32[64]{0:T(128)} %param.35) | copy-start | bytes 772
